TPU v7x, 128 devices: a whole 4x4x4 slice. The times are simulated.
128 devices in a mesh: tm: 4 (over x), space: 32 (over y, z, core).
Axes of the slice: x: 4, y: 4, z: 4, core: 2. Of those that a mesh axis runs over, the one named last changes fastest.
Arguments:
- dual_weights: float32 [1048576], P(('tm', 'space')), may hold values from -6 to 6
- direction: float32 [1048576], P(('tm', 'space')), may hold values from -20 to 20
- residual_dual: float32 [1048576], P(('tm', 'space')), may hold values from -20 to 20
- obs_var: float32 [1048576], P(('tm', 'space')), may hold values from 0.2 to 1
- obs_route: int32 [1048576, 1], P(('tm', 'space')), may hold values from 0 to 127; in each aligned block of 8192 rows (0 to 8191, 8192 to 16383, ...) at most 128 rows name the same one
- obs_cell: int32 [1048576], P(('tm', 'space')), may hold values from 0 to 524030, as said below
- obs_interp: float32 [4, 1048576], P(None, ('tm', 'space')), may hold values from 0 to 1, as said below
- wind_x: float32 [4, 16, 256, 256], P('tm', None, 'space'), may hold values from -0.35 to 0.35
- wind_y: float32 [4, 16, 256, 256], P('tm', None, 'space'), may hold values from -0.35 to 0.35
- coupling: float32 [4, 4], replicated, may hold values from -3 to 3
- cov_scale: float32 [4, 4, 16], P('tm'), may hold values from 1.5 to 4
Outputs:
- dual_next: float32 [1048576], P(('tm', 'space'))
- residual_next: float32 [1048576], P(('tm', 'space'))
- direction_next: float32 [1048576], P(('tm', 'space'))
Inputs may be any that keep to these rules, and one draw needn't show every extreme that they name: `obs_route`: among the rows of one device, at most 128 observations name any one destination. `obs_cell`: A cell (step, variable, level, x, y) of the destination strip with x below 7 and y below 255. `obs_interp`: four nonnegative bilinear weights summing to one for each observation.
All inputs are finite; a program needn't handle non-finite values.
Results may differ from a plain program's by a relative error of at most 0.0001.
Values sent between devices are 32-bit elements; how exact they have to be, the bound alone decides.
A program may use at most 128 MiB of HBM per device.

v0:
```python
import jax
import jax.numpy as jnp
from jax import lax
from jax.sharding import PartitionSpec as P

STEPS = 4


diffusion = 0.05
vertical = 0.05
coupling_step = 0.05


def with_halo(cells, sides, width):
    for axis, dim in sides:
        count = lax.axis_size(axis)
        ends = count - 1
        head = lax.slice_in_dim(cells, 0, width, axis=dim)
        tail = lax.slice_in_dim(cells, cells.shape[dim] - width, cells.shape[dim], axis=dim)
        cells = jnp.concatenate(
            [
                lax.ppermute(tail, axis, [(i, (i + 1) % count) for i in range(ends)]),
                cells,
                lax.ppermute(head, axis, [((i + 1) % count, i) for i in range(ends)]),
            ],
            axis=dim,
        )
    return cells


def from_behind(block, axis, distance):
    devices = range(lax.axis_size(axis))
    route = [(i - distance, i) for i in devices if i - distance in devices]
    return lax.ppermute(block, axis, route)


def neighbour(grid_field, axis_no, offset):
    extent = grid_field.shape[axis_no]
    widths = [(1, 1) if dim_no == axis_no else (0, 0) for dim_no in range(grid_field.ndim)]
    padded = jnp.pad(grid_field, widths)
    return lax.slice_in_dim(padded, 1 + offset, 1 + offset + extent, axis=axis_no)


def coefficients(wind_east, wind_north):
    west_weight = jnp.maximum(wind_east, 0.0) + diffusion
    east_weight = jnp.maximum(-wind_east, 0.0) + diffusion
    south_weight = jnp.maximum(wind_north, 0.0) + diffusion
    north_weight = jnp.maximum(-wind_north, 0.0) + diffusion
    centre = 1.0 - jnp.abs(wind_east) - jnp.abs(wind_north) - 4.0 * diffusion - 2.0 * vertical
    return (centre, west_weight, east_weight, south_weight, north_weight)


def forward_step(model_state, weights_tuple, coupling):
    centre, west_weight, east_weight, south_weight, north_weight = weights_tuple
    padded = with_halo(model_state, (("space", 2),), 1)
    result = centre * model_state + west_weight * padded[:, :, :-2] + east_weight * padded[:, :, 2:]
    result = (
        result
        + south_weight * neighbour(model_state, 3, -1)
        + north_weight * neighbour(model_state, 3, 1)
    )
    result = result + vertical * (neighbour(model_state, 1, -1) + neighbour(model_state, 1, 1))
    return result + coupling_step * jnp.einsum(
        "vw,wlxy->vlxy", coupling, model_state, precision=lax.Precision.HIGHEST
    )


def adjoint_step(model_state, weights_tuple, west_outer, east_outer, coupling):
    centre, west_weight, east_weight, south_weight, north_weight = weights_tuple
    padded = with_halo(model_state, (("space", 2),), 1)
    result = (
        centre * model_state
        + west_outer[:, 1:] * padded[:, :, 2:]
        + east_outer[:, :-1] * padded[:, :, :-2]
    )
    result = (
        result
        + neighbour(south_weight * model_state, 3, 1)
        + neighbour(north_weight * model_state, 3, -1)
    )
    result = result + vertical * (neighbour(model_state, 1, -1) + neighbour(model_state, 1, 1))
    return result + coupling_step * jnp.einsum(
        "wv,wlxy->vlxy", coupling, model_state, precision=lax.Precision.HIGHEST
    )


def smooth_padded(padded):
    return 0.5 * padded[:, :, 1:-1] + 0.25 * (padded[:, :, :-2] + padded[:, :, 2:])


def smooth_local(grid_field, axis_no):
    return 0.5 * grid_field + 0.25 * (
        neighbour(grid_field, axis_no, -1) + neighbour(grid_field, axis_no, 1)
    )


def per_device(
    dual_weights,
    direction,
    residual_dual,
    obs_var,
    obs_route,
    obs_cell,
    obs_interp,
    wind_x,
    wind_y,
    coupling,
    cov_scale,
):
    n_time = lax.axis_size("tm")
    n_space = lax.axis_size("space")
    devices = n_time * n_space
    own_rows = direction.shape[0]
    capacity = 2 * own_rows // devices
    levels = wind_x.shape[1]
    strip_width = wind_x.shape[2]
    columns = wind_x.shape[3]
    variables = coupling.shape[0]
    my_group = lax.axis_index("tm")
    targets = obs_route[:, 0]
    one_hot = (targets[:, None] == jnp.arange(devices, dtype=jnp.int32)[None, :]).astype(jnp.int32)
    ranking = jnp.sum((jnp.cumsum(one_hot, axis=0) - one_hot) * one_hot, axis=1)
    slot_index = targets * capacity + ranking
    payload = jnp.concatenate([direction[None, :], obs_interp], axis=0)
    outgoing = jnp.zeros((5, devices * capacity), jnp.float32).at[:, slot_index].set(payload)
    cells_sent = jnp.zeros((devices * capacity,), jnp.int32).at[slot_index].set(obs_cell)
    arrived = lax.all_to_all(
        outgoing.reshape(5, devices, capacity),
        ("tm", "space"),
        split_axis=1,
        concat_axis=1,
        tiled=True,
    )
    cells_in = lax.all_to_all(
        cells_sent.reshape(devices, capacity),
        ("tm", "space"),
        split_axis=0,
        concat_axis=0,
        tiled=True,
    )
    arrived = arrived.reshape(5, devices * capacity)
    cells_in = cells_in.reshape(devices * capacity)
    corner_index = jnp.concatenate(
        [cells_in, cells_in + columns, cells_in + 1, cells_in + columns + 1]
    )
    corner_weight = arrived[1:].reshape(-1)
    spread_direction = jnp.concatenate([arrived[0], arrived[0], arrived[0], arrived[0]])
    cell_count = STEPS * variables * levels * strip_width * columns
    forcing = (
        jnp.zeros((cell_count,), jnp.float32).at[corner_index].add(corner_weight * spread_direction)
    )
    forcing = forcing.reshape(STEPS, variables, levels, strip_width, columns)
    weights_tuple = coefficients(wind_x[0], wind_y[0])
    state_shape = (variables, levels, strip_width, columns)
    west_next = from_behind(weights_tuple[1][:, :1, :], "space", -1)
    east_prev = from_behind(weights_tuple[2][:, -1:, :], "space", 1)
    west_outer = jnp.concatenate([weights_tuple[1], west_next], axis=1)
    east_outer = jnp.concatenate([east_prev, weights_tuple[2]], axis=1)
    incoming = jnp.zeros(state_shape, jnp.float32)
    keeper = jnp.zeros(state_shape, jnp.float32)
    for section_index in range(n_time):
        current = incoming
        for step_index in reversed(range(STEPS)):
            current = adjoint_step(
                current + forcing[step_index], weights_tuple, west_outer, east_outer, coupling
            )
        keeper = jnp.where(my_group == n_time - 1 - section_index, current, keeper)
        if section_index + 1 < n_time:
            incoming = from_behind(current, "tm", -1)
    scales = cov_scale[0][:, :, None, None]
    scaled = scales * keeper
    padded = with_halo(scaled, (("space", 2),), 1)
    once = smooth_padded(padded)
    padded_again = with_halo(once, (("space", 2),), 1)
    twice = smooth_padded(padded_again)
    twice = smooth_local(smooth_local(twice, 3), 3)
    increment = scales * twice
    incoming = jnp.zeros(state_shape, jnp.float32)
    kept_states = jnp.zeros((STEPS,) + state_shape, jnp.float32)
    for section_index in range(n_time):
        current = incoming + increment
        trail = []
        for step_index in range(STEPS):
            current = forward_step(current, weights_tuple, coupling)
            trail.append(current)
        kept_states = jnp.where(my_group == section_index, jnp.stack(trail), kept_states)
        if section_index + 1 < n_time:
            incoming = from_behind(current, "tm", 1)
    flat_states = kept_states.reshape(-1)
    sampled = flat_states[corner_index].reshape(4, devices * capacity)
    mapped_slots = jnp.sum(arrived[1:] * sampled, axis=0)
    returned = lax.all_to_all(
        mapped_slots.reshape(devices, capacity),
        ("tm", "space"),
        split_axis=0,
        concat_axis=0,
        tiled=True,
    )
    mapped = returned.reshape(devices * capacity)[slot_index]
    image = mapped + obs_var * direction
    norm_now, curvature = lax.psum(
        (jnp.sum(residual_dual * residual_dual), jnp.sum(direction * image)), ("tm", "space")
    )
    step_size = norm_now / curvature
    residual_next = residual_dual - step_size * image
    norm_next = lax.psum(jnp.sum(residual_next * residual_next), ("tm", "space"))
    dual_next = dual_weights + step_size * direction
    direction_next = residual_next + norm_next / norm_now * direction
    return (dual_next, residual_next, direction_next)


def solution(mesh):
    return jax.shard_map(
        per_device,
        mesh=mesh,
        in_specs=(
            P(("tm", "space")),
            P(("tm", "space")),
            P(("tm", "space")),
            P(("tm", "space")),
            P(("tm", "space"), None),
            P(("tm", "space")),
            P(None, ("tm", "space")),
            P("tm", None, "space", None),
            P("tm", None, "space", None),
            P(),
            P("tm", None, None),
        ),
        out_specs=(P(("tm", "space")), P(("tm", "space")), P(("tm", "space"))),
        check_vma=False,
    )
```

profile of v0, /device:TPU:1, one launch (start us, length us, event | category | flops | bytes accessed | tf_op | source)
XLA Modules:
  0.0 1593.6 jit_solution(16173608835285116973)
XLA Ops:
  12.9 31.2 %scatter_custom_fusion.1 = s32[16384]{0:T(1024)} fusion(s32[8192]{0:T(1024)S(1)} %bitcast.390, s32[8192]{0:T(1024)} %param.16, s32[]{:T(128)} %constant.19.clone.1), kind=kCustom, calls=%fused_computation.721 | custom fusion | bytes 66048 | tf_op jit(solution)/shard_map/scatter | solution.py:126
  44.2 11.5 all-to-all-start.1
  65.5 24.7 %scatter_custom_fusion = f32[5,16384]{0,1:T(8,128)} fusion(s32[8192]{0:T(1024)S(1)} %bitcast.391, f32[8192,5]{1,0:T(8,128)} %copy.81, f32[]{:T(128)} %constant.17.clone.1), kind=kCustom, calls=%fused_computation.12 | custom fusion | bytes 328192 | tf_op jit(solution)/shard_map/scatter | solution.py:125
  96.8 10.1 all-to-all-start
  107.3 13.1 all-to-all-done
  120.7 358.8 %scatter_custom_fusion.2 = f32[524288]{0:T(1024)S(1)} fusion(s32[65536]{0:T(1024)S(1)} %bitcast.365, f32[65536]{0:T(1024)S(1)} %maximum_multiply_fusion, f32[]{:T(128)} %constant.17.clone.1), kind=kCustom, calls=%fused_computation.132 | custom fusion | flops 65536 | bytes 2097156 | tf_op jit(solution)/shard_map/scatter-add | solution.py:150
  484.1 36.5 %collective-permute-start.1 = (f32[4,16,1,256]{3,0,2,1:T(4,128)}, f32[4,16,1,256]{3,0,2,1:T(4,128)}, u32[]{:S(2)}, u32[]{:S(2)}) collective-permute-start(f32[4,16,1,256]{3,0,2,1:T(4,128)} %get-tuple-element.107), channel_id=1, source_target_pairs={{1,0},{2,1},{3,2},{4,3},{5,4},{6,5},{7,6},{8,7},{9,8},{10,9},{11,1... | collective-permute-start | bytes 196616 | tf_op jit(solution)/shard_map/ppermute | solution.py:24
  520.7 33.9 %collective-permute-start.3 = (f32[4,16,1,256]{3,0,2,1:T(4,128)S(1)}, f32[4,16,1,256]{3,0,2,1:T(4,128)}, u32[]{:S(2)}, u32[]{:S(2)}) collective-permute-start(f32[4,16,1,256]{3,0,2,1:T(4,128)S(1)} %get-tuple-element.108), channel_id=1, source_target_pairs={{0,1},{1,2},{2,3},{3,4},{4,5},{5,6},{6,7},{7,8},{8,9},{9,10},{10,1... | collective-permute-start | bytes 196616 | tf_op jit(solution)/shard_map/ppermute | solution.py:22
  596.8 12.0 collective-permute-done.10
  650.5 12.4 collective-permute-done.19
  704.5 12.4 collective-permute-done.28
  719.4 6.8 collective-permute-start.30
  780.3 8.0 collective-permute-done.40
  795.7 9.2 collective-permute-done.42
  811.7 9.7 collective-permute-done.44
  848.0 8.1 collective-permute-done.49
  908.2 8.1 collective-permute-done.58
  968.7 7.9 collective-permute-done.67
  1028.4 362.7 %gather_fusion = f32[65536]{0:T(1024)S(1)} fusion(f32[524288]{0:T(1024)S(1)} %bitcast.361, s32[65536]{0:T(1024)S(1)} %broadcast_clamp_fusion), kind=kCustom, calls=%fused_computation | custom fusion | bytes 786432 | tf_op jit(solution)/shard_map/gather | solution.py:190
  1391.8 16.0 %all-to-all-start.2 = ((f32[128,1,128]{2,1,0:T(1,128)}), f32[128,1,128]{2,1,0:T(1,128)S(1)}, u32[]{:S(2)}, u32[]{:S(2)}) async-start(f32[128,1,128]{2,1,0:T(1,128)} %bitcast.92), calls=%async_computation.2 | async-start | bytes 131072 | tf_op jit(solution)/shard_map/all_to_all | solution.py:192
  1407.9 9.3 all-to-all-done.2
  1417.2 45.5 %gather_fusion.1 = f32[8192]{0:T(1024)S(1)} fusion(f32[16384]{0:T(1024)S(1)} %bitcast.362, s32[8192]{0:T(1024)S(1)} %broadcast_clamp_fusion.1), kind=kCustom, calls=%fused_computation.1 | custom fusion | bytes 98304 | tf_op jit(solution)/shard_map/gather | solution.py:199
  1463.4 63.2 %all-reduce.82 = (f32[]{:T(128)}, f32[]{:T(128)}) all-reduce(f32[]{:T(128)} %get-tuple-element.135, f32[]{:T(128)} %get-tuple-element.134), channel_id=1, replica_groups=mesh['tm'=4,'space'=32] {'tm','space'}, use_global_device_ids=true, to_apply=%region_1.2 | all-reduce | flops 2 | bytes 16 | tf_op jit(solution)/shard_map/psum | solution.py:201
  1528.6 62.6 %psum.23 = f32[]{:T(128)} all-reduce(f32[]{:T(128)} %get-tuple-element.5), channel_id=1, replica_groups=mesh['tm'=4,'space'=32] {'tm','space'}, use_global_device_ids=true, to_apply=%region_12.13 | all-reduce | flops 1 | bytes 8 | tf_op jit(solution)/shard_map/psum | solution.py:206
  (331 shorter events, 414.0 us)
Async XLA Ops:
  44.2 52.7 %all-to-all-start.1 = ((s32[128,1,128]{2,1,0:T(1,128)}), s32[128,1,128]{2,1,0:T(1,128)S(1)}, u32[]{:S(2)}, u32[]{:S(2)}) async-start(s32[128,1,128]{2,1,0:T(1,128)} %bitcast.12), calls=%async_computation.1 | async-start | bytes 131072 | tf_op jit(solution)/shard_map/all_to_all | solution.py:134
  56.5 39.7 %collective-permute-start.2 = (f32[16,1,256]{2,1,0:T(1,128)S(1)}, f32[16,1,256]{2,1,0:T(1,128)S(1)}, u32[]{:S(2)}, u32[]{:S(2)}) collective-permute-start(f32[16,1,256]{2,1,0:T(1,128)S(1)} %slice.1295), channel_id=1, source_target_pairs={{0,1},{1,2},{2,3},{3,4},{4,5},{5,6},{6,7},{7,8},{8,9},{9,10},{10,1... | collective-permute-start | bytes 49160 | tf_op jit(solution)/shard_map/ppermute | solution.py:34
  60.7 493.9 %collective-permute-start = (f32[16,1,256]{2,1,0:T(1,128)}, f32[16,1,256]{2,1,0:T(1,128)}, u32[]{:S(2)}, u32[]{:S(2)}) collective-permute-start(f32[16,1,256]{2,1,0:T(1,128)} %slice.1293), channel_id=1, source_target_pairs={{1,0},{2,1},{3,2},{4,3},{5,4},{6,5},{7,6},{8,7},{9,8},{10,9},{11,1... | collective-permute-start | bytes 49160 | tf_op jit(solution)/shard_map/ppermute | solution.py:34
  96.8 23.6 %all-to-all-start = ((f32[5,128,128]{2,0,1:T(8,128)}), f32[5,128,128]{2,0,1:T(8,128)S(1)}, u32[]{:S(2)}, u32[]{:S(2)}) async-start(f32[5,128,128]{2,0,1:T(8,128)} %copy.82), calls=%async_computation | async-start | bytes 1048576 | tf_op jit(solution)/shard_map/all_to_all | solution.py:127
  484.1 72.1 %collective-permute-start.1 = (f32[4,16,1,256]{3,0,2,1:T(4,128)}, f32[4,16,1,256]{3,0,2,1:T(4,128)}, u32[]{:S(2)}, u32[]{:S(2)}) collective-permute-start(f32[4,16,1,256]{3,0,2,1:T(4,128)} %get-tuple-element.107), channel_id=1, source_target_pairs={{1,0},{2,1},{3,2},{4,3},{5,4},{6,5},{7,6},{8,7},{9,8},{10,9},{11,1... | collective-permute-start | bytes 196616 | tf_op jit(solution)/shard_map/ppermute | solution.py:24
  520.7 35.5 %collective-permute-start.3 = (f32[4,16,1,256]{3,0,2,1:T(4,128)S(1)}, f32[4,16,1,256]{3,0,2,1:T(4,128)}, u32[]{:S(2)}, u32[]{:S(2)}) collective-permute-start(f32[4,16,1,256]{3,0,2,1:T(4,128)S(1)} %get-tuple-element.108), channel_id=1, source_target_pairs={{0,1},{1,2},{2,3},{3,4},{4,5},{5,6},{6,7},{7,8},{8,9},{9,10},{10,1... | collective-permute-start | bytes 196616 | tf_op jit(solution)/shard_map/ppermute | solution.py:22
  595.0 13.9 collective-permute-start.10
  649.2 13.7 collective-permute-start.19
  703.2 13.7 collective-permute-start.28
  717.5 8.9 collective-permute-start.29
  719.4 8.1 collective-permute-start.30
  778.3 9.9 collective-permute-start.40
  793.7 11.2 collective-permute-start.42
  809.8 11.7 collective-permute-start.44
  836.9 7.7 collective-permute-start.48
  846.7 9.4 collective-permute-start.49
  882.8 7.7 collective-permute-start.55
  894.6 7.7 collective-permute-start.57
  904.4 12.0 collective-permute-start.58
  954.8 7.7 collective-permute-start.66
  964.6 12.0 collective-permute-start.67
  1003.3 7.8 collective-permute-start.73
  1015.2 7.7 collective-permute-start.75
  1391.8 25.4 %all-to-all-start.2 = ((f32[128,1,128]{2,1,0:T(1,128)}), f32[128,1,128]{2,1,0:T(1,128)S(1)}, u32[]{:S(2)}, u32[]{:S(2)}) async-start(f32[128,1,128]{2,1,0:T(1,128)} %bitcast.92), calls=%async_computation.2 | async-start | bytes 131072 | tf_op jit(solution)/shard_map/all_to_all | solution.py:192
  (91 other events, 3649.0 us)
where the time goes:
time: 1600 us; the launch traced here: 1590 us
  local copies, waits for them, and re-layouts  485 us (30%)
  other arithmetic  381 us (24%)
  starting transfers between devices  310 us (19%)
  waiting for transfers between devices  206 us (13%)
  blocking collectives  126 us (8%)
  matrix products  80.4 us (5%)
    gather x1, local copies, waits for them, and re-layouts, per_device(): sampled = flat_states[corner_index].reshape(4, devices * capacity)  363 us
    scatter-add x1, other arithmetic, per_device(): jnp.zeros((cell_count,), jnp.float32).at[corner_index]  359 us
    ppermute x34, starting transfers between devices, with_halo(): lax.ppermute(tail, axis, [(i, (i + 1) % count) for i in range(ends)])  148 us
    ppermute x34, starting transfers between devices, with_halo(): lax.ppermute(head, axis, [((i + 1) % count, i) for i in range(ends)])  106 us
    ppermute x34, waiting for transfers between devices, with_halo(): lax.ppermute(head, axis, [((i + 1) % count, i) for i in range(ends)])  104 us
    psum x1, blocking collectives, per_device(): lax.psum((jnp.sum(residual_dual * residual_dual), jnp.sum(direction * ima...  63.2 us
    psum x1, blocking collectives, per_device(): lax.psum(jnp.sum(residual_next * residual_next), ('tm', 'space'))  62.6 us
    ppermute x8, waiting for transfers between devices, from_behind(): return lax.ppermute(block, axis, route)  60.9 us
  transfers between devices with their start and end apart: 79, of which 41 were waited for; matrix products, arithmetic and copies ran while one was open for 25% of the time, Pallas kernels for 0%

commit v1 on v0

v1 whole, which is shorter than its diff:
```python
import functools

import jax
import jax.numpy as jnp
from jax import lax
from jax.experimental import pallas as pl
from jax.experimental.pallas import tpu as pltpu
from jax.sharding import PartitionSpec as P

STEPS = 4
NV = 4
LEV = 16
CX = 8
NY = 256
CAP = 128
ROWS = LEV * CX
BUCKETS = STEPS * NV
SORT_ROWS = 160
CHUNK = 1024
SUB = 256
DELAY = 3
diffusion = 0.05
vertical = 0.05
coupling_step = 0.05
MESH = pl.DeviceIdType.MESH
F32 = jnp.float32
BF16 = jnp.bfloat16
VMEM = pl.BlockSpec(memory_space=pltpu.VMEM)
SMEM = pl.BlockSpec(memory_space=pltpu.SMEM)


def params(mib, **kw):
    return pltpu.CompilerParams(vmem_limit_bytes=mib * 1024 * 1024, **kw)


def iota(shape, dim):
    return lax.broadcasted_iota(jnp.int32, shape, dim)


def parts_of(value, count):
    out = []
    for _ in range(count - 1):
        head = value.astype(BF16)
        out.append(head)
        value = value - head.astype(F32)
    out.append(value.astype(BF16))
    return out


def nt(a, b):
    return lax.dot_general(a, b, (((1,), (1,)), ((), ())), preferred_element_type=F32)


def nn(a, b):
    return jnp.dot(a, b, preferred_element_type=F32)


def one_hot(mask):
    return jnp.where(mask, 1.0, 0.0).astype(BF16)


def running_rank(hot, hot_mask, carry, upper):
    keys = hot.shape[0]
    pieces = CHUNK // SUB
    stacked = jnp.concatenate([hot[:, i * SUB : (i + 1) * SUB] for i in range(pieces)], axis=0)
    counted = nn(stacked, upper)
    rows = []
    for i in range(pieces):
        mask = hot_mask[:, i * SUB : (i + 1) * SUB]
        part = counted[i * keys : (i + 1) * keys] + carry
        rows.append(jnp.sum(jnp.where(mask, part, 0.0), axis=0, keepdims=True))
        carry = carry + jnp.sum(jnp.where(mask, 1.0, 0.0), axis=1, keepdims=True)
    return jnp.concatenate(rows, axis=1), carry


def upper_strict():
    return one_hot(iota((SUB, SUB), 0) < iota((SUB, SUB), 1))


PACK_PARTS = (3, 2, 2, 2, 2, 2, 2, 2)


def pack_kernel(route_ref, field_ref, out_ref, rank_ref, acc_ref):
    devices = out_ref.shape[0]
    upper = upper_strict()
    acc_ref[...] = jnp.zeros_like(acc_ref)

    def body(c, carry):
        lanes = pl.ds(pl.multiple_of(c * CHUNK, CHUNK), CHUNK)
        dest = route_ref[:, lanes]
        mask = iota((devices, CHUNK), 0) == dest
        hot = one_hot(mask)
        rank, carry = running_rank(hot, mask, carry, upper)
        rank = rank.astype(jnp.int32)
        rank_ref[:, lanes] = rank
        slot = one_hot(iota((CAP, CHUNK), 0) == rank)
        fields = field_ref[:, lanes]
        pieces = []
        for f, count in enumerate(PACK_PARTS):
            for part in parts_of(fields[f : f + 1], count):
                pieces.append(slot * part)
        acc_ref[...] += nt(hot, jnp.concatenate(pieces, axis=0))
        return carry

    lax.fori_loop(0, route_ref.shape[1] // CHUNK, body, jnp.zeros((devices, 1), F32))
    at = 0
    for f, count in enumerate(PACK_PARTS):
        total = acc_ref[:, at * CAP : (at + 1) * CAP]
        for i in range(1, count):
            total = total + acc_ref[:, (at + i) * CAP : (at + i + 1) * CAP]
        at += count
        out_ref[:, f, :] = total


def row_of(ref, field, c):
    per = CHUNK // CAP
    base = c * per
    return jnp.concatenate([ref[base + i, field : field + 1, :] for i in range(per)], axis=1)


SORT_PARTS = 12


def sort_scatter_kernel(recv_ref, forcing_ref, sorted_ref, pos_ref, start_ref, rank_ref, acc_ref):
    chunks = recv_ref.shape[0] * CAP // CHUNK
    upper = upper_strict()

    def bucket_of(c):
        cell = row_of(recv_ref, 0, c).astype(jnp.int32) - 1
        bucket = jnp.where(cell < 0, -1, cell // (ROWS * NY))
        return cell, iota((BUCKETS, CHUNK), 0) == bucket

    def count_body(c, carry):
        _, mask = bucket_of(c)
        rank, carry = running_rank(one_hot(mask), mask, carry, upper)
        rank_ref[pl.ds(c, 1), :] = rank
        return carry

    totals = lax.fori_loop(0, chunks, count_body, jnp.zeros((BUCKETS, 1), F32))
    tiles = jnp.floor((totals + (SUB - 1.0)) * (1.0 / SUB))
    before = jnp.zeros((BUCKETS, 1), F32)
    ids = iota((BUCKETS, 1), 0)
    for b in range(BUCKETS):
        here = jnp.sum(jnp.where(ids == b, tiles, 0.0))
        before = before + jnp.where(ids > b, here, 0.0)
    for b in range(BUCKETS):
        start_ref[0, b] = jnp.sum(jnp.where(ids == b, before, 0.0)).astype(jnp.int32)
    start_ref[0, BUCKETS] = jnp.sum(tiles).astype(jnp.int32)
    offsets = before * float(SUB)

    acc_ref[...] = jnp.zeros_like(acc_ref)

    def sort_body(c, carry):
        cell, mask = bucket_of(c)
        offset = jnp.sum(jnp.where(mask, offsets, 0.0), axis=0, keepdims=True)
        pos = (offset + rank_ref[pl.ds(c, 1), :]).astype(jnp.int32)
        pos = jnp.where(cell < 0, -1, pos)
        pos_ref[pl.ds(c, 1), :] = pos
        high = one_hot(iota((SORT_ROWS, CHUNK), 0) == (pos >> 7))
        low = one_hot(iota((CAP, CHUNK), 0) == (pos & 127))
        inside = (cell & (ROWS * NY - 1)).astype(F32)
        pieces = []
        for value in [inside] + [row_of(recv_ref, f, c) for f in range(1, 6)]:
            for part in parts_of(value, 2):
                pieces.append(low * part)
        acc_ref[...] += nt(high, jnp.concatenate(pieces, axis=0))
        return carry

    lax.fori_loop(0, chunks, sort_body, 0)
    for f in range(SORT_PARTS // 2):
        sorted_ref[f] = (
            acc_ref[:, 2 * f * CAP : (2 * f + 1) * CAP]
            + acc_ref[:, (2 * f + 1) * CAP : (2 * f + 2) * CAP]
        )

    def bucket_body(b, carry):
        def tile_body(t, total):
            def row(f):
                return jnp.concatenate(
                    [sorted_ref[f, pl.ds(2 * t, 1), :], sorted_ref[f, pl.ds(2 * t + 1, 1), :]],
                    axis=1,
                )

            cell = row(0).astype(jnp.int32)
            hot = one_hot(iota((ROWS, SUB), 0) == (cell >> 8))
            y = cell & (NY - 1)
            spots = iota((NY, SUB), 0)
            here = one_hot(spots == y)
            above = one_hot(spots == y + 1)
            d = row(5)
            w = [parts_of(row(1 + i) * d, 2) for i in range(4)]
            stacked = jnp.concatenate(
                [
                    jnp.concatenate([here * w[0][p] + above * w[2][p] for p in range(2)], axis=1),
                    jnp.concatenate([here * w[1][p] + above * w[3][p] for p in range(2)], axis=1),
                ],
                axis=0,
            )
            return total + nt(jnp.concatenate([hot, hot], axis=1), stacked)

        total = lax.fori_loop(
            start_ref[0, b], start_ref[0, b + 1], tile_body, jnp.zeros((ROWS, 2 * NY), F32)
        )
        forcing_ref[b] = total[:, :NY] + pltpu.roll(total[:, NY:], 1, 0)
        return carry

    lax.fori_loop(0, BUCKETS, bucket_body, 0)


def gather_kernel(
    start_ref, state_ref, sorted_ref, pos_ref, recv_ref, own_ref, out_ref, value_ref
):
    devices = recv_ref.shape[0]
    chunks = devices * CAP // CHUNK
    value_ref[...] = jnp.zeros_like(value_ref)

    def bucket_body(b, carry):
        turned = state_ref[b].T
        shifted = pltpu.roll(turned, ROWS - 1, 1)
        table = jnp.concatenate(
            [
                jnp.concatenate(parts_of(turned, 2), axis=1),
                jnp.concatenate(parts_of(shifted, 2), axis=1),
            ],
            axis=0,
        )

        def tile_body(t, carry):
            def row(f):
                return jnp.concatenate(
                    [sorted_ref[f, pl.ds(2 * t, 1), :], sorted_ref[f, pl.ds(2 * t + 1, 1), :]],
                    axis=1,
                )

            cell = row(0).astype(jnp.int32)
            hot = one_hot(iota((ROWS, SUB), 0) == (cell >> 8))
            y = cell & (NY - 1)
            spots = iota((NY, SUB), 0)
            here = spots == y
            above = spots == y + 1
            got = nn(table, jnp.concatenate([hot, hot], axis=0))
            first = jnp.where(here, row(1), jnp.where(above, row(3), 0.0))
            second = jnp.where(here, row(2), jnp.where(above, row(4), 0.0))
            value = jnp.sum(first * got[:NY] + second * got[NY:], axis=0, keepdims=True)
            value_ref[pl.ds(2 * t, 1), :] = value[:, :CAP]
            value_ref[pl.ds(2 * t + 1, 1), :] = value[:, CAP:]
            return carry

        return lax.fori_loop(start_ref[0, b], start_ref[0, b + 1], tile_body, carry)

    lax.fori_loop(0, BUCKETS, bucket_body, 0)
    table = jnp.concatenate(parts_of(value_ref[...].T, 2), axis=1)
    depth = value_ref.shape[0]

    def unsort_body(c, carry):
        pos = pos_ref[pl.ds(c, 1), :]
        high = one_hot(iota((depth, CHUNK), 0) == (pos >> 7))
        got = nn(table, jnp.concatenate([high, high], axis=0))
        low = iota((CAP, CHUNK), 0) == (pos & 127)
        row = jnp.sum(jnp.where(low, got, 0.0), axis=0, keepdims=True)
        per = CHUNK // CAP
        block = jnp.concatenate([row[:, i * CAP : (i + 1) * CAP] for i in range(per)], axis=0)
        out_ref[pl.ds(pl.multiple_of(c * per, per), per), :CAP] = block
        return carry

    lax.fori_loop(0, chunks, unsort_body, 0)
    d = recv_ref[:, 5, :]
    r = recv_ref[:, 6, :]
    image = out_ref[:, :CAP] + recv_ref[:, 7, :] * d
    out_ref[:, :CAP] = image
    own = own_ref[...]
    lane = iota((1, CAP), 1)
    sums = jnp.where(lane == 0, jnp.sum(own * own), 0.0)
    sums = jnp.where(lane == 1, jnp.sum(d * image), sums)
    sums = jnp.where(lane == 2, jnp.sum(r * image), sums)
    sums = jnp.where(lane == 3, jnp.sum(image * image), sums)
    out_ref[:, CAP:] = jnp.broadcast_to(sums, (devices, CAP))


def final_kernel(
    back_ref, route_ref, rank_ref, dual_ref, d_ref, r_ref, dual_out, res_out, dir_out
):
    devices = back_ref.shape[0]
    sums = jnp.sum(back_ref[:, CAP:], axis=0, keepdims=True)
    lane = iota((1, CAP), 1)
    norm_now, curvature, cross, square = [
        jnp.sum(jnp.where(lane == i, sums, 0.0), axis=1, keepdims=True) for i in range(4)
    ]
    step = norm_now / curvature
    norm_next = norm_now - 2.0 * step * cross + step * step * square
    ratio = norm_next / norm_now
    table = jnp.concatenate(parts_of(back_ref[:, :CAP].T, 2), axis=1)
    for c in range(route_ref.shape[0]):
        hot = one_hot(iota((devices, CHUNK), 0) == route_ref[c : c + 1, :])
        got = nn(table, jnp.concatenate([hot, hot], axis=0))
        mask = iota((CAP, CHUNK), 0) == rank_ref[c : c + 1, :]
        image = jnp.sum(jnp.where(mask, got, 0.0), axis=0, keepdims=True)
        d = d_ref[c : c + 1, :]
        res = r_ref[c : c + 1, :] - step * image
        dual_out[c : c + 1, :] = dual_ref[c : c + 1, :] + step * d
        res_out[c : c + 1, :] = res
        dir_out[c : c + 1, :] = res + ratio * d


EXT = CX + 8


def pack_four(dst, value, lo):
    for v in range(NV):
        dst[v // 2, (v % 2) * 4 : (v % 2) * 4 + 4, :] = value[v][lo : lo + 4]


def pack_two(dst, value, lo):
    for v in range(NV):
        dst[2 * v : 2 * v + 2, :] = value[v][lo : lo + 2]


def sweep_kernel(
    forcing_ref,
    wind_ref,
    coupling_ref,
    scale_ref,
    state_ref,
    wind_in,
    coef,
    hop_a,
    hop_x,
    fin_a,
    fin_x,
    halo_out,
    halo_in,
    cov_out,
    cov_in,
    fwd_out,
    fwd_in,
    fext,
    u0,
    u1,
    u2,
    u3,
    inc,
    wind_sem,
    hop_sem,
    halo_sem,
    cov_sem,
    fwd_sem,
):
    g = lax.axis_index("tm")
    t = lax.axis_index("space")
    groups = lax.axis_size("tm")
    strips = lax.axis_size("space")
    left = (g, lax.rem(t + strips - 1, strips))
    right = (g, lax.rem(t + 1, strips))
    later = (lax.rem(g + 1, groups), t)
    earlier = (lax.rem(g + groups - 1, groups), t)
    sides = (left, right)
    first_strip = t == 0
    last_strip = t == strips - 1
    last_group = g == groups - 1
    first_group = g == 0

    barrier = pltpu.get_barrier_semaphore()
    for other in (left, right, later, earlier):
        pl.semaphore_signal(barrier, inc=1, device_id=other, device_id_type=MESH)
    pl.semaphore_wait(barrier, 4)

    def to_side(src, dst, sems, side, *idx):
        return pltpu.make_async_remote_copy(
            src_ref=src,
            dst_ref=dst,
            send_sem=sems.at[(0, side) + idx],
            recv_sem=sems.at[(1, 1 - side) + idx],
            device_id=sides[side],
            device_id_type=MESH,
        )

    def wait_side(dst, sems, slot, *idx):
        pltpu.make_async_remote_copy(
            src_ref=dst,
            dst_ref=dst,
            send_sem=sems.at[(0, slot) + idx],
            recv_sem=sems.at[(1, slot) + idx],
            device_id=sides[slot],
            device_id_type=MESH,
        ).wait_recv()

    def hop(src, dst, way, level, device):
        return pltpu.make_async_remote_copy(
            src_ref=src.at[level],
            dst_ref=dst.at[level],
            send_sem=hop_sem.at[way, 0, level],
            recv_sem=hop_sem.at[way, 1, level],
            device_id=device,
            device_id_type=MESH,
        )

    for side in range(2):
        to_side(wind_ref, wind_in.at[1 - side], wind_sem, side).start()

    edge = jnp.zeros((NV, EXT, NY), F32)
    for u in (u0, u1, u2, u3):
        u[0] = edge
        u[LEV + 1] = edge

    @pl.when(last_group)
    def _():
        hop_a[...] = jnp.zeros_like(hop_a)

    @pl.when(first_group)
    def _():
        hop_x[...] = jnp.zeros_like(hop_x)

    for slot in range(2):
        wait_side(wind_in.at[slot], wind_sem, slot)

    column = iota((EXT, NY), 0)
    lane = iota((EXT, NY), 1)
    low_x = jnp.where(first_strip, 4, 0)
    high_x = jnp.where(last_strip, 11, 15)
    inside = (column >= low_x) & (column <= high_x)
    west_ok = inside & ((column > 4) | jnp.logical_not(first_strip))
    east_ok = inside & ((column < 11) | jnp.logical_not(last_strip))
    south_ok = inside & (lane > 0)
    north_ok = inside & (lane < NY - 1)

    def coef_body(l, carry):
        winds = []
        for i in range(2):
            winds.append(
                jnp.concatenate(
                    [wind_in[0, i, l, 4:8], wind_ref[i, l], wind_in[1, i, l, 0:4]], axis=0
                )
            )
        wx, wy = winds
        coef[0, l] = jnp.where(
            inside, 1.0 - jnp.abs(wx) - jnp.abs(wy) - 4.0 * diffusion - 2.0 * vertical, 0.0
        )
        coef[1, l] = jnp.where(west_ok, jnp.maximum(wx, 0.0) + diffusion, 0.0)
        coef[2, l] = jnp.where(east_ok, jnp.maximum(-wx, 0.0) + diffusion, 0.0)
        coef[3, l] = jnp.where(south_ok, jnp.maximum(wy, 0.0) + diffusion, 0.0)
        coef[4, l] = jnp.where(north_ok, jnp.maximum(-wy, 0.0) + diffusion, 0.0)
        return carry

    lax.fori_loop(0, LEV, coef_body, 0)

    mix = [[coupling_step * coupling_ref[v, w] for w in range(NV)] for v in range(NV)]

    def adjoint_level(u, l):
        c, w, e, s, n = [coef[i, l] for i in range(5)]
        now = [u[l + 1, v] for v in range(NV)]
        out = []
        for v in range(NV):
            a = now[v]
            res = c * a + pltpu.roll(w * a, EXT - 1, 0) + pltpu.roll(e * a, 1, 0)
            res = res + pltpu.roll(s * a, NY - 1, 1) + pltpu.roll(n * a, 1, 1)
            res = res + vertical * (u[l, v] + u[l + 2, v])
            for k in range(NV):
                res = res + mix[k][v] * now[k]
            out.append(res)
        return out

    def forward_level(u, l):
        c, w, e, s, n = [coef[i, l] for i in range(5)]
        now = [u[l + 1, v] for v in range(NV)]
        out = []
        for v in range(NV):
            a = now[v]
            res = c * a + w * pltpu.roll(a, 1, 0) + e * pltpu.roll(a, EXT - 1, 0)
            res = res + s * pltpu.roll(a, 1, 1) + n * pltpu.roll(a, NY - 1, 1)
            res = res + vertical * (u[l, v] + u[l + 2, v])
            for k in range(NV):
                res = res + mix[v][k] * now[k]
            out.append(res)
        return out

    def in_range(l):
        return (l >= 0) & (l < LEV)

    def adjoint_tick(k, carry):
        @pl.when(k < LEV)
        def _():
            @pl.when(jnp.logical_not(last_group))
            def _():
                hop(hop_a, hop_a, 0, k, later).wait_recv()

            value = [hop_a[k, v] + forcing_ref[3, v, k] for v in range(NV)]
            for v in range(NV):
                u0[k + 1, v, 4 : 4 + CX] = value[v]
            for side in range(2):
                lo = 4 * side
                buf = halo_out.at[side, k]
                pack_four(buf.at[0:2], value, lo)
                pack_four(buf.at[2:4], [forcing_ref[2, v, k] for v in range(NV)], lo)
                lo = 6 * side
                pack_two(buf.at[4], [forcing_ref[1, v, k] for v in range(NV)], lo)
                pack_two(buf.at[5], [forcing_ref[0, v, k] for v in range(NV)], lo)
                to_side(buf, halo_in.at[1 - side, k], halo_sem, side, k).start()

        m = k - DELAY

        @pl.when(in_range(m))
        def _():
            for slot in range(2):
                wait_side(halo_in.at[slot, m], halo_sem, slot, m)
            for v in range(NV):
                rows = slice((v % 2) * 4, (v % 2) * 4 + 4)
                pair = slice(2 * v, 2 * v + 2)
                u0[m + 1, v, 0:4] = halo_in[0, m, v // 2, rows]
                u0[m + 1, v, 12:16] = halo_in[1, m, v // 2, rows]
                fext[2, m, v, 0:4] = halo_in[0, m, 2 + v // 2, rows]
                fext[2, m, v, 12:16] = halo_in[1, m, 2 + v // 2, rows]
                fext[2, m, v, 4:12] = forcing_ref[2, v, m]
                for i, tile in ((1, 4), (0, 5)):
                    fext[i, m, v, 0:2] = jnp.zeros((2, NY), F32)
                    fext[i, m, v, 14:16] = jnp.zeros((2, NY), F32)
                    fext[i, m, v, 2:4] = halo_in[0, m, tile, pair]
                    fext[i, m, v, 12:14] = halo_in[1, m, tile, pair]
                    fext[i, m, v, 4:12] = forcing_ref[i, v, m]

        for i, (src, dst) in enumerate(((u0, u1), (u1, u2), (u2, u3))):
            level = m - 1 - i

            @pl.when(in_range(level))
            def _():
                res = adjoint_level(src, level)
                for v in range(NV):
                    dst[level + 1, v] = res[v] + fext[2 - i, level, v]

        level = m - 4

        @pl.when(in_range(level))
        def _():
            res = [r[4 : 4 + CX] for r in adjoint_level(u3, level)]
            for v in range(NV):
                fin_a[level, v] = res[v]

            @pl.when(jnp.logical_not(first_group))
            def _():
                hop(fin_a, hop_a, 0, level, earlier).start()

            for side in range(2):
                pack_two(cov_out.at[side, level], res, 6 * side)
                to_side(
                    cov_out.at[side, level], cov_in.at[1 - side, level], cov_sem, side, level
                ).start()

        return carry

    lax.fori_loop(0, LEV + DELAY + 4, adjoint_tick, 0)

    lane_low = jnp.where(iota((CX, NY), 1) > 0, 1.0, 0.0)
    lane_high = jnp.where(iota((CX, NY), 1) < NY - 1, 1.0, 0.0)
    keep = jnp.where(inside, 1.0, 0.0)

    def cov_level(l, carry):
        for slot in range(2):
            wait_side(cov_in.at[slot, l], cov_sem, slot, l)
        zero = jnp.zeros((2, NY), F32)
        for v in range(NV):
            pair = slice(2 * v, 2 * v + 2)
            scale = scale_ref[v, l]
            ext = jnp.concatenate(
                [zero, cov_in[0, l, pair], fin_a[l, v], cov_in[1, l, pair], zero], axis=0
            )
            ext = ext * (keep * scale)
            ext = 0.5 * ext + 0.25 * (pltpu.roll(ext, 1, 0) + pltpu.roll(ext, EXT - 1, 0))
            ext = ext * keep
            ext = 0.5 * ext + 0.25 * (pltpu.roll(ext, 1, 0) + pltpu.roll(ext, EXT - 1, 0))
            own = ext[4 : 4 + CX]
            for _ in range(2):
                own = 0.5 * own + 0.25 * (
                    lane_low * pltpu.roll(own, 1, 1) + lane_high * pltpu.roll(own, NY - 1, 1)
                )
            inc[l, v] = own * scale
        return carry

    lax.fori_loop(0, LEV, cov_level, 0)

    def forward_tick(k, carry):
        @pl.when(k < LEV)
        def _():
            @pl.when(jnp.logical_not(first_group))
            def _():
                hop(hop_x, hop_x, 1, k, earlier).wait_recv()

            value = [hop_x[k, v] + inc[k, v] for v in range(NV)]
            for v in range(NV):
                u0[k + 1, v, 4 : 4 + CX] = value[v]
            for side in range(2):
                buf = fwd_out.at[side, k]
                pack_four(buf, value, 4 * side)
                to_side(buf, fwd_in.at[1 - side, k], fwd_sem, side, k).start()

        m = k - DELAY

        @pl.when(in_range(m))
        def _():
            for slot in range(2):
                wait_side(fwd_in.at[slot, m], fwd_sem, slot, m)
            for v in range(NV):
                rows = slice((v % 2) * 4, (v % 2) * 4 + 4)
                u0[m + 1, v, 0:4] = fwd_in[0, m, v // 2, rows]
                u0[m + 1, v, 12:16] = fwd_in[1, m, v // 2, rows]

        for i, (src, dst) in enumerate(((u0, u1), (u1, u2), (u2, u3))):
            level = m - 1 - i

            @pl.when(in_range(level))
            def _():
                res = forward_level(src, level)
                for v in range(NV):
                    dst[level + 1, v] = res[v]
                    state_ref[i, v, level] = res[v][4 : 4 + CX]

        level = m - 4

        @pl.when(in_range(level))
        def _():
            res = [r[4 : 4 + CX] for r in forward_level(u3, level)]
            for v in range(NV):
                state_ref[3, v, level] = res[v]
                fin_x[level, v] = res[v]

            @pl.when(jnp.logical_not(last_group))
            def _():
                hop(fin_x, hop_x, 1, level, later).start()

        return carry

    lax.fori_loop(0, LEV + DELAY + 4, forward_tick, 0)

    for side in range(2):
        to_side(wind_ref, wind_in.at[1 - side], wind_sem, side).wait_send()

    def drain(l, carry):
        for side in range(2):
            to_side(halo_out.at[side, l], halo_in.at[1 - side, l], halo_sem, side, l).wait_send()
            to_side(cov_out.at[side, l], cov_in.at[1 - side, l], cov_sem, side, l).wait_send()
            to_side(fwd_out.at[side, l], fwd_in.at[1 - side, l], fwd_sem, side, l).wait_send()

        @pl.when(jnp.logical_not(first_group))
        def _():
            hop(fin_a, hop_a, 0, l, earlier).wait_send()

        @pl.when(jnp.logical_not(last_group))
        def _():
            hop(fin_x, hop_x, 1, l, later).wait_send()

        return carry

    lax.fori_loop(0, LEV, drain, 0)


def sweeps(forcing, winds, coupling, scale):
    state = (LEV, NV, CX, NY)
    padded = (LEV + 2, NV, EXT, NY)
    dma = pltpu.SemaphoreType.DMA
    return pl.pallas_call(
        sweep_kernel,
        out_shape=jax.ShapeDtypeStruct((STEPS, NV, LEV, CX, NY), F32),
        in_specs=[VMEM, VMEM, SMEM, SMEM],
        out_specs=VMEM,
        scratch_shapes=[
            pltpu.VMEM((2, 2, LEV, CX, NY), F32),
            pltpu.VMEM((5, LEV, EXT, NY), F32),
            pltpu.VMEM(state, F32),
            pltpu.VMEM(state, F32),
            pltpu.VMEM(state, F32),
            pltpu.VMEM(state, F32),
            pltpu.VMEM((2, LEV, 6, 8, NY), F32),
            pltpu.VMEM((2, LEV, 6, 8, NY), F32),
            pltpu.VMEM((2, LEV, 8, NY), F32),
            pltpu.VMEM((2, LEV, 8, NY), F32),
            pltpu.VMEM((2, LEV, 2, 8, NY), F32),
            pltpu.VMEM((2, LEV, 2, 8, NY), F32),
            pltpu.VMEM((3, LEV, NV, EXT, NY), F32),
            pltpu.VMEM(padded, F32),
            pltpu.VMEM(padded, F32),
            pltpu.VMEM(padded, F32),
            pltpu.VMEM(padded, F32),
            pltpu.VMEM(state, F32),
            dma((2, 2)),
            dma((2, 2, LEV)),
            dma((2, 2, LEV)),
            dma((2, 2, LEV)),
            dma((2, 2, LEV)),
        ],
        compiler_params=params(48, collective_id=1, has_side_effects=True),
        name="sweeps",
    )(forcing, winds, coupling, scale)


def per_device(
    dual_weights,
    direction,
    residual_dual,
    obs_var,
    obs_route,
    obs_cell,
    obs_interp,
    wind_x,
    wind_y,
    coupling,
    cov_scale,
):
    devices = lax.axis_size("tm") * lax.axis_size("space")
    rows = direction.shape[0]
    wide = (rows // CHUNK, CHUNK)
    route = obs_route.reshape(1, rows)
    fields = jnp.concatenate(
        [
            (obs_cell + 1).astype(F32)[None],
            obs_interp,
            direction[None],
            residual_dual[None],
            obs_var[None],
        ],
        axis=0,
    )
    outgoing, rank = pl.pallas_call(
        pack_kernel,
        out_shape=(
            jax.ShapeDtypeStruct((devices, 8, CAP), F32),
            jax.ShapeDtypeStruct((1, rows), jnp.int32),
        ),
        in_specs=[VMEM, VMEM],
        out_specs=(VMEM, VMEM),
        scratch_shapes=[pltpu.VMEM((devices, sum(PACK_PARTS) * CAP), F32)],
        compiler_params=params(48),
        name="pack",
    )(route, fields)
    arrived = lax.all_to_all(outgoing, ("tm", "space"), split_axis=0, concat_axis=0, tiled=True)
    slots = devices * CAP
    forcing, ordered, position, starts = pl.pallas_call(
        sort_scatter_kernel,
        out_shape=(
            jax.ShapeDtypeStruct((BUCKETS, ROWS, NY), F32),
            jax.ShapeDtypeStruct((SORT_PARTS // 2, SORT_ROWS, CAP), F32),
            jax.ShapeDtypeStruct((slots // CHUNK, CHUNK), jnp.int32),
            jax.ShapeDtypeStruct((1, BUCKETS + 1), jnp.int32),
        ),
        in_specs=[VMEM],
        out_specs=(VMEM, VMEM, VMEM, SMEM),
        scratch_shapes=[
            pltpu.VMEM((slots // CHUNK, CHUNK), F32),
            pltpu.VMEM((SORT_ROWS, SORT_PARTS * CAP), F32),
        ],
        compiler_params=params(48),
        name="sort_scatter",
    )(arrived)
    winds = jnp.concatenate([wind_x, wind_y], axis=0)
    states = sweeps(
        forcing.reshape(STEPS, NV, LEV, CX, NY), winds, coupling, cov_scale[0]
    )
    returning = pl.pallas_call(
        gather_kernel,
        out_shape=jax.ShapeDtypeStruct((devices, 2 * CAP), F32),
        in_specs=[SMEM, VMEM, VMEM, VMEM, VMEM, VMEM],
        out_specs=VMEM,
        scratch_shapes=[pltpu.VMEM((256, CAP), F32)],
        compiler_params=params(48),
        name="gather",
    )(
        starts,
        states.reshape(BUCKETS, ROWS, NY),
        ordered,
        position,
        arrived,
        residual_dual.reshape(wide),
    )
    back = lax.all_to_all(returning, ("tm", "space"), split_axis=0, concat_axis=0, tiled=True)
    out = jax.ShapeDtypeStruct(wide, F32)
    results = pl.pallas_call(
        final_kernel,
        out_shape=(out, out, out),
        in_specs=[VMEM] * 6,
        out_specs=(VMEM, VMEM, VMEM),
        compiler_params=params(48),
        name="final",
    )(
        back,
        route.reshape(wide),
        rank.reshape(wide),
        dual_weights.reshape(wide),
        direction.reshape(wide),
        residual_dual.reshape(wide),
    )
    return tuple(r.reshape(rows) for r in results)


def solution(mesh):
    return jax.shard_map(
        per_device,
        mesh=mesh,
        in_specs=(
            P(("tm", "space")),
            P(("tm", "space")),
            P(("tm", "space")),
            P(("tm", "space")),
            P(("tm", "space"), None),
            P(("tm", "space")),
            P(None, ("tm", "space")),
            P("tm", None, "space", None),
            P("tm", None, "space", None),
            P(),
            P("tm", None, None),
        ),
        out_specs=(P(("tm", "space")), P(("tm", "space")), P(("tm", "space"))),
        check_vma=False,
    )
```

time: 1600 us -> 270 us (0.17)
  local copies, waits for them, and re-layouts: 485 us -> 5.34 us
  other arithmetic: 381 us -> 2.28 us
  starting transfers between devices: 310 us -> 64.5 us
  waiting for transfers between devices: 206 us -> 20.5 us
  Pallas kernels: 0 us -> 176 us
  blocking collectives: 126 us -> 0 us
  matrix products: 80.4 us -> 0 us
    gather x2 -> x0, local copies, waits for them, and re-layouts: 408 us -> none  [the longest x1 363 us: per_device(): sampled = flat_states[corner_index].reshape(4, devices * capacity)]
    scatter-add x1 -> x0, other arithmetic: 359 us -> none  [per_device(): jnp.zeros((cell_count,), jnp.float32).at[corner_index]]
    ppermute x76 -> x0, starting transfers between devices: 273 us -> none  [the longest x34 148 us: with_halo(): lax.ppermute(tail, axis, [(i, (i + 1) % count) for i in range(ends)])]
    ppermute x76 -> x0, waiting for transfers between devices: 184 us -> none  [the longest x34 104 us: with_halo(): lax.ppermute(head, axis, [((i + 1) % count, i) for i in range(ends)])]
    pallas_call x0 -> x5, Pallas kernels: none -> 176 us  [the longest x1 108 us: sweeps(): pl.pallas_call(sweep_kernel, out_shape=jax.ShapeDtypeStruct((STEPS, NV, L...]
    psum x2 -> x0, blocking collectives: 126 us -> none  [the longest x1 63.2 us: per_device(): lax.psum((jnp.sum(residual_dual * residual_dual), jnp.sum(direction * ima...]
    dot_general x32 -> x0, matrix products: 80.4 us -> none  [the longest x16 46.9 us: adjoint_step(): jnp.einsum('wv,wlxy->vlxy', coupling, model_state, precision=lax.Precisio...]
    scatter x2 -> x0, local copies, waits for them, and re-layouts: 55.9 us -> none  [the longest x1 31.2 us: per_device(): jnp.zeros((devices * capacity,), jnp.int32).at[slot_index].set(obs_cell)]
  transfers between devices with their start and end apart: 79 -> 2, of which waited for: 41 -> 2; matrix products, arithmetic and copies ran while one was open for 25% -> 1% of each run, Pallas kernels for 0% -> 0%
where the time goes in v1:
time: 270 us
  Pallas kernels  176 us (65%)
  starting transfers between devices  64.5 us (24%)
  waiting for transfers between devices  20.5 us (8%)
  local copies, waits for them, and re-layouts  5.34 us (2%)
    pallas_call x1, Pallas kernels, sweeps(): pl.pallas_call(sweep_kernel, out_shape=jax.ShapeDtypeStruct((STEPS, NV, L...  108 us
    all_to_all x1, starting transfers between devices, per_device(): lax.all_to_all(returning, ('tm', 'space'), split_axis=0, concat_axis=0, t...  53 us
    pallas_call x1, Pallas kernels, per_device(): pl.pallas_call(sort_scatter_kernel, out_shape=(jax.ShapeDtypeStruct((BUCK...  33.9 us
    pallas_call x1, Pallas kernels, per_device(): pl.pallas_call(gather_kernel, out_shape=jax.ShapeDtypeStruct((devices, 2...  17 us
    pallas_call x1, Pallas kernels, per_device(): pl.pallas_call(pack_kernel, out_shape=(jax.ShapeDtypeStruct((devices, 8,...  15.9 us
    all_to_all x1, waiting for transfers between devices, per_device(): lax.all_to_all(outgoing, ('tm', 'space'), split_axis=0, concat_axis=0, ti...  12.9 us
    all_to_all x1, starting transfers between devices, per_device(): lax.all_to_all(outgoing, ('tm', 'space'), split_axis=0, concat_axis=0, ti...  11.5 us
    all_to_all x1, waiting for transfers between devices, per_device(): lax.all_to_all(returning, ('tm', 'space'), split_axis=0, concat_axis=0, t...  7.68 us
  transfers between devices with their start and end apart: 2, of which 2 were waited for; matrix products, arithmetic and copies ran while one was open for 1% of the time, Pallas kernels for 0%

profile of v1, /device:TPU:1, one launch (start us, length us, event | category | flops | bytes accessed | tf_op | source)
XLA Modules:
  0.0 269.7 jit_solution(1466566882969118449)
XLA Ops:
  0.7 0.8 add_convert_fusion
  1.5 1.2 concatenate.6.field_ref
  2.7 0.0 copy-start
  2.7 0.7 copy-done
  3.4 15.9 %pack.1 = (f32[128,8,128]{2,1,0:T(8,128)}, s32[1,8192]{1,0:T(1,128)S(1)}) custom-call(s32[1,8192]{1,0:T(1,128)S(1)} %bitcast.27, f32[8,8192]{1,0:T(8,128)S(1)} %concatenate.6.field_ref), custom_call_target="tpu_custom_call" | custom-call | tf_op jit(solution)/shard_map/pack/pallas_call | solution.py:720
  19.3 11.5 %all-to-all-start = ((f32[128,8,128]{2,1,0:T(8,128)}), f32[128,8,128]{2,1,0:T(8,128)S(1)}, u32[]{:S(2)}, u32[]{:S(2)}) async-start(f32[128,8,128]{2,1,0:T(8,128)} %get-tuple-element.12), calls=%async_computation | async-start | bytes 1048576 | tf_op jit(solution)/shard_map/all_to_all | solution.py:732
  30.8 0.8 reshape.42.own_ref.r_ref
  31.7 12.9 %all-to-all-done.recv_ref = f32[128,8,128]{2,1,0:T(8,128)S(1)} async-done(((f32[128,8,128]{2,1,0:T(8,128)}), f32[128,8,128]{2,1,0:T(8,128)S(1)}, u32[]{:S(2)}, u32[]{:S(2)}) %all-to-all-start) | async-done | bytes 524320 | tf_op jit(solution)/shard_map/all_to_all | solution.py:732
  44.5 33.9 %sort_scatter.1 = (f32[16,128,256]{2,1,0:T(8,128)S(1)}, f32[6,160,128]{2,1,0:T(8,128)S(1)}, s32[16,1024]{1,0:T(8,128)S(1)}, s32[1,17]{1,0:T(1,128)S(1)}) custom-call(f32[128,8,128]{2,1,0:T(8,128)S(1)} %all-to-all-done.recv_ref), custom_call_target="tpu_custom_call" | custom-call | tf_op jit(solution)/shard_map/sort_scatter/pallas_call | solution.py:734
  78.5 0.0 copy-done.3
  78.5 107.7 %sweeps.1 = f32[4,4,16,8,256]{4,3,2,1,0:T(8,128)S(1)} custom-call(f32[4,4,16,8,256]{4,3,2,1,0:T(8,128)S(1)} %bitcast.24, f32[2,16,8,256]{3,2,1,0:T(8,128)S(1)} %pad_maximum_fusion.wind_ref, f32[4,4]{1,0:T(4,128)S(1)} %copy-done.2, f32[4,16]{1,0:T(4,128)S(1)} %bitcast.31), custom_call_target="tpu_custom_call" | custom-call | tf_op jit(solution)/shard_map/sweeps/pallas_call | solution.py:658
  186.2 0.0 copy-start.4
  186.2 0.0 copy-start.1
  186.3 0.0 copy-start.7
  186.3 17.0 %gather.1 = f32[128,256]{1,0:T(8,128)S(1)} custom-call(s32[1,17]{1,0:T(1,128)S(1)} %get-tuple-element.13.start_ref, f32[16,128,256]{2,1,0:T(8,128)S(1)} %bitcast.23, f32[6,160,128]{2,1,0:T(8,128)S(1)} %get-tuple-element.15.sorted_ref, s32[16,1024]{1,0:T(8,128)S(1)} %get-tuple-element.16.pos_ref, f32[128,8,128]{2,1,0:T(8,128)S(1)} %all-to-all-done.recv_ref, ...), custom_call_target="tpu_custom_call" | custom-call | tf_op jit(solution)/shard_map/gather/pallas_call | solution.py:755
  203.3 0.8 copy.14
  204.1 53.0 %all-to-all-start.1 = ((f32[128,1,256]{2,1,0:T(1,128)}), f32[128,1,256]{2,1,0:T(1,128)S(1)}, u32[]{:S(2)}, u32[]{:S(2)}) async-start(f32[128,1,256]{2,1,0:T(1,128)} %copy.14), calls=%async_computation.1 | async-start | bytes 262144 | tf_op jit(solution)/shard_map/all_to_all | solution.py:771
  257.2 0.5 broadcast.6
  257.7 0.7 reduce.6
  258.4 0.7 reduce.7
  259.2 7.7 %all-to-all-done.1 = f32[128,1,256]{2,1,0:T(1,128)S(1)} async-done(((f32[128,1,256]{2,1,0:T(1,128)}), f32[128,1,256]{2,1,0:T(1,128)S(1)}, u32[]{:S(2)}, u32[]{:S(2)}) %all-to-all-start.1) | async-done | bytes 131104 | tf_op jit(solution)/shard_map/all_to_all | solution.py:771
  266.9 1.6 final.1
  268.4 0.6 copy.24
  269.1 0.6 copy_bitcast_fusion.1
  (16 shorter events, 0.1 us)
Async XLA Ops:
  0.6 31.0 %copy-start.6 = (f32[1,16,8,256]{3,2,1,0:T(8,128)S(1)}, f32[1,16,8,256]{3,2,1,0:T(8,128)}, u32[]{:S(2)}) copy-start(f32[1,16,8,256]{3,2,1,0:T(8,128)} %param.18) | copy-start | bytes 393220
  0.6 31.0 %copy-start.5 = (f32[1,16,8,256]{3,2,1,0:T(8,128)S(1)}, f32[1,16,8,256]{3,2,1,0:T(8,128)}, u32[]{:S(2)}) copy-start(f32[1,16,8,256]{3,2,1,0:T(8,128)} %param.19) | copy-start | bytes 393220
  0.7 77.8 %copy-start.3 = (f32[1,4,16]{2,1,0:T(4,128)S(1)}, f32[1,4,16]{2,1,0:T(4,128)}, u32[]{:S(2)}) copy-start(f32[1,4,16]{2,1,0:T(4,128)} %param.21) | copy-start | bytes 772
  0.7 77.8 %copy-start.2 = (f32[4,4]{1,0:T(4,128)S(1)}, f32[4,4]{1,0:T(4,128)}, u32[]{:S(2)}) copy-start(f32[4,4]{1,0:T(4,128)} %coupling_ref.1) | copy-start | bytes 196
  2.7 0.8 copy-start
  19.3 25.2 %all-to-all-start = ((f32[128,8,128]{2,1,0:T(8,128)}), f32[128,8,128]{2,1,0:T(8,128)S(1)}, u32[]{:S(2)}, u32[]{:S(2)}) async-start(f32[128,8,128]{2,1,0:T(8,128)} %get-tuple-element.12), calls=%async_computation | async-start | bytes 1048576 | tf_op jit(solution)/shard_map/all_to_all | solution.py:732
  186.2 70.9 %copy-start.4 = (f32[8192]{0:T(1024)S(1)}, f32[8192]{0:T(1024)}, u32[]{:S(2)}) copy-start(f32[8192]{0:T(1024)} %param.12) | copy-start | bytes 98308
  186.2 71.4 %copy-start.1 = (s32[8192,1]{0,1:T(1,128)S(1)}, s32[8192,1]{0,1:T(1,128)}, u32[]{:S(2)}) copy-start(s32[8192,1]{0,1:T(1,128)} %param.15) | copy-start | bytes 98308
  186.3 72.9 %copy-start.7 = (f32[8192]{0:T(1024)S(1)}, f32[8192]{0:T(1024)}, u32[]{:S(2)}) copy-start(f32[8192]{0:T(1024)} %param.11) | copy-start | bytes 98308
  204.1 62.8 %all-to-all-start.1 = ((f32[128,1,256]{2,1,0:T(1,128)}), f32[128,1,256]{2,1,0:T(1,128)S(1)}, u32[]{:S(2)}, u32[]{:S(2)}) async-start(f32[128,1,256]{2,1,0:T(1,128)} %copy.14), calls=%async_computation.1 | async-start | bytes 262144 | tf_op jit(solution)/shard_map/all_to_all | solution.py:771

commit v2 on v1

--- a/solution.py
+++ b/solution.py
@@ -18,7 +18,12 @@
 SORT_ROWS = 160
 CHUNK = 1024
 SUB = 256
-DELAY = 3
+HALF = NY // 2
+EXT = 2 * CX
+ADJ_DELAY = 5
+COV_DELAY = 5
+FWD_DELAY = 5
+FIRST_DELAY = 5
 diffusion = 0.05
 vertical = 0.05
 coupling_step = 0.05
@@ -73,6 +78,10 @@
     return jnp.concatenate(rows, axis=1), carry
 
 
+def lane_of(y):
+    return (y >> 1) + (y & 1) * HALF
+
+
 def upper_strict():
     return one_hot(iota((SUB, SUB), 0) < iota((SUB, SUB), 1))
 
@@ -80,7 +89,100 @@
 PACK_PARTS = (3, 2, 2, 2, 2, 2, 2, 2)
 
 
-def pack_kernel(route_ref, field_ref, out_ref, rank_ref, acc_ref):
+def everyone(me, act):
+    g = lax.axis_index("tm")
+    t = lax.axis_index("space")
+    groups = lax.axis_size("tm")
+    strips = lax.axis_size("space")
+    for step in range(groups):
+        group = g + step
+        group = jnp.where(group >= groups, group - groups, group)
+
+        def body(i, carry):
+            strip = t + i
+            strip = jnp.where(strip >= strips, strip - strips, strip)
+            act(group * strips + strip, (group, strip))
+            return carry
+
+        lax.fori_loop(0 if step else 1, strips, body, 0, unroll=True)
+
+
+def greet_all(me):
+    barrier = pltpu.get_barrier_semaphore()
+    everyone(
+        me,
+        lambda peer, device: pl.semaphore_signal(
+            barrier, inc=1, device_id=device, device_id_type=MESH
+        ),
+    )
+
+
+def await_all():
+    devices = lax.axis_size("tm") * lax.axis_size("space")
+    pl.semaphore_wait(pltpu.get_barrier_semaphore(), devices - 1)
+
+
+def send_all(me, out, arrived, send_sem, recv_sem):
+    def start(peer, device):
+        pltpu.make_async_remote_copy(
+            src_ref=out.at[peer],
+            dst_ref=arrived.at[me],
+            send_sem=send_sem,
+            recv_sem=recv_sem,
+            device_id=device,
+            device_id_type=MESH,
+        ).start()
+
+    pltpu.make_async_copy(out.at[me], arrived.at[me], recv_sem).start()
+    everyone(me, start)
+
+
+def receive_all(arrived, recv_sem):
+    pltpu.make_async_copy(arrived, arrived, recv_sem).wait()
+
+
+def finish_sends(out, send_sem):
+    rest = out.at[pl.ds(0, out.shape[0] - 1)]
+    pltpu.make_async_copy(rest, rest, send_sem).wait()
+
+
+def my_index():
+    return lax.axis_index("tm") * lax.axis_size("space") + lax.axis_index("space")
+
+
+def route_kernel(
+    route_ref,
+    field_ref,
+    wind_ref,
+    arrived_ref,
+    rank_ref,
+    coef,
+    out_ref,
+    landing,
+    acc_ref,
+    wind_own,
+    wind_in,
+    send_sem,
+    recv_sem,
+    wind_sem,
+):
+    me = my_index()
+    g = lax.axis_index("tm")
+    t = lax.axis_index("space")
+    strips = lax.axis_size("space")
+    sides = ((g, lax.rem(t + strips - 1, strips)), (g, lax.rem(t + 1, strips)))
+    first_strip = t == 0
+    last_strip = t == strips - 1
+    greet_all(me)
+
+    order = iota((NY, NY), 1)
+    order = one_hot(iota((NY, NY), 0) == (order % HALF) * 2 + order // HALF)
+    rows = 2 * LEV * CX
+    turned = parts_of(wind_ref[...].reshape(rows, NY), 3)
+    wind_own[...] = (nn(turned[0], order) + nn(turned[1], order) + nn(turned[2], order)).reshape(
+        2, LEV, CX, NY
+    )
+
     devices = out_ref.shape[0]
     upper = upper_strict()
     acc_ref[...] = jnp.zeros_like(acc_ref)
@@ -111,6 +213,65 @@
         at += count
         out_ref[:, f, :] = total
 
+    await_all()
+
+    def to_side(side):
+        return pltpu.make_async_remote_copy(
+            src_ref=wind_own,
+            dst_ref=wind_in.at[1 - side],
+            send_sem=wind_sem.at[0, side],
+            recv_sem=wind_sem.at[1, 1 - side],
+            device_id=sides[side],
+            device_id_type=MESH,
+        )
+
+    send_all(me, out_ref, landing, send_sem, recv_sem)
+    for side in range(2):
+        to_side(side).start()
+    for side in range(2):
+        to_side(side).wait_recv()
+
+    column = iota((EXT, NY), 0)
+    lane = iota((EXT, NY), 1)
+    west_ok = jnp.logical_not(first_strip & (column == 0))
+    east_ok = jnp.logical_not(last_strip & (column == CX - 1))
+    inside = inside_grid(first_strip, last_strip)
+    west_ok = inside & west_ok
+    east_ok = inside & east_ok
+    south_ok = inside & (lane > 0)
+    north_ok = inside & (lane < NY - 1)
+    from_right = iota((CX, NY), 0) < 4
+
+    def coef_body(l, carry):
+        wx, wy = [
+            jnp.concatenate(
+                [wind_own[i, l], jnp.where(from_right, wind_in[1, i, l], wind_in[0, i, l])], axis=0
+            )
+            for i in range(2)
+        ]
+        coef[0, l] = jnp.where(
+            inside, 1.0 - jnp.abs(wx) - jnp.abs(wy) - 4.0 * diffusion - 2.0 * vertical, 0.0
+        )
+        coef[1, l] = jnp.where(west_ok, jnp.maximum(wx, 0.0) + diffusion, 0.0)
+        coef[2, l] = jnp.where(east_ok, jnp.maximum(-wx, 0.0) + diffusion, 0.0)
+        coef[3, l] = jnp.where(south_ok, jnp.maximum(wy, 0.0) + diffusion, 0.0)
+        coef[4, l] = jnp.where(north_ok, jnp.maximum(-wy, 0.0) + diffusion, 0.0)
+        return carry
+
+    lax.fori_loop(0, LEV, coef_body, 0)
+    receive_all(landing, recv_sem)
+    arrived_ref[...] = landing[...]
+    for side in range(2):
+        to_side(side).wait_send()
+    finish_sends(out_ref, send_sem)
+
+
+def inside_grid(first_strip, last_strip):
+    column = iota((EXT, NY), 0)
+    return jnp.logical_not(
+        (first_strip & (column >= 12)) | (last_strip & (column >= 8) & (column < 12))
+    )
+
 
 def row_of(ref, field, c):
     per = CHUNK // CAP
@@ -185,8 +346,8 @@
             hot = one_hot(iota((ROWS, SUB), 0) == (cell >> 8))
             y = cell & (NY - 1)
             spots = iota((NY, SUB), 0)
-            here = one_hot(spots == y)
-            above = one_hot(spots == y + 1)
+            here = one_hot(spots == lane_of(y))
+            above = one_hot(spots == lane_of(y + 1))
             d = row(5)
             w = [parts_of(row(1 + i) * d, 2) for i in range(4)]
             stacked = jnp.concatenate(
@@ -236,8 +397,8 @@
             hot = one_hot(iota((ROWS, SUB), 0) == (cell >> 8))
             y = cell & (NY - 1)
             spots = iota((NY, SUB), 0)
-            here = spots == y
-            above = spots == y + 1
+            here = spots == lane_of(y)
+            above = spots == lane_of(y + 1)
             got = nn(table, jnp.concatenate([hot, hot], axis=0))
             first = jnp.where(here, row(1), jnp.where(above, row(3), 0.0))
             second = jnp.where(here, row(2), jnp.where(above, row(4), 0.0))
@@ -278,10 +439,27 @@
 
 
 def final_kernel(
-    back_ref, route_ref, rank_ref, dual_ref, d_ref, r_ref, dual_out, res_out, dir_out
+    out_ref,
+    route_ref,
+    rank_ref,
+    dual_ref,
+    d_ref,
+    r_ref,
+    dual_out,
+    res_out,
+    dir_out,
+    landing,
+    send_sem,
+    recv_sem,
 ):
-    devices = back_ref.shape[0]
-    sums = jnp.sum(back_ref[:, CAP:], axis=0, keepdims=True)
+    devices = out_ref.shape[0]
+    me = my_index()
+    greet_all(me)
+    await_all()
+    send_all(me, out_ref, landing, send_sem, recv_sem)
+    receive_all(landing, recv_sem)
+    returned = landing[...].reshape(devices, 2 * CAP)
+    sums = jnp.sum(returned[:, CAP:], axis=0, keepdims=True)
     lane = iota((1, CAP), 1)
     norm_now, curvature, cross, square = [
         jnp.sum(jnp.where(lane == i, sums, 0.0), axis=1, keepdims=True) for i in range(4)
@@ -289,7 +467,7 @@
     step = norm_now / curvature
     norm_next = norm_now - 2.0 * step * cross + step * step * square
     ratio = norm_next / norm_now
-    table = jnp.concatenate(parts_of(back_ref[:, :CAP].T, 2), axis=1)
+    table = jnp.concatenate(parts_of(returned[:, :CAP].T, 2), axis=1)
     for c in range(route_ref.shape[0]):
         hot = one_hot(iota((devices, CHUNK), 0) == route_ref[c : c + 1, :])
         got = nn(table, jnp.concatenate([hot, hot], axis=0))
@@ -300,35 +478,31 @@
         dual_out[c : c + 1, :] = dual_ref[c : c + 1, :] + step * d
         res_out[c : c + 1, :] = res
         dir_out[c : c + 1, :] = res + ratio * d
-
-
-EXT = CX + 8
-
-
-def pack_four(dst, value, lo):
-    for v in range(NV):
-        dst[v // 2, (v % 2) * 4 : (v % 2) * 4 + 4, :] = value[v][lo : lo + 4]
-
-
-def pack_two(dst, value, lo):
-    for v in range(NV):
-        dst[2 * v : 2 * v + 2, :] = value[v][lo : lo + 2]
+    finish_sends(out_ref, send_sem)
+
+
+def back(x):
+    return jnp.concatenate([pltpu.roll(x[:, HALF:], 1, 1), x[:, :HALF]], axis=1)
+
+
+def ahead(x):
+    return jnp.concatenate([x[:, HALF:], pltpu.roll(x[:, :HALF], HALF - 1, 1)], axis=1)
 
 
 def sweep_kernel(
     forcing_ref,
-    wind_ref,
+    coef,
     coupling_ref,
     scale_ref,
     state_ref,
-    wind_in,
-    coef,
     hop_a,
     hop_x,
     fin_a,
     fin_x,
-    halo_out,
-    halo_in,
+    adj_out,
+    adj_in,
+    force_out,
+    force_in,
     cov_out,
     cov_in,
     fwd_out,
@@ -338,10 +512,14 @@
     u1,
     u2,
     u3,
+    v0,
+    v1,
+    v2,
+    v3,
     inc,
-    wind_sem,
     hop_sem,
-    halo_sem,
+    adj_sem,
+    force_sem,
     cov_sem,
     fwd_sem,
 ):
@@ -362,6 +540,7 @@
     barrier = pltpu.get_barrier_semaphore()
     for other in (left, right, later, earlier):
         pl.semaphore_signal(barrier, inc=1, device_id=other, device_id_type=MESH)
+
     pl.semaphore_wait(barrier, 4)
 
     def to_side(src, dst, sems, side, *idx):
@@ -394,11 +573,41 @@
             device_id_type=MESH,
         )
 
-    for side in range(2):
-        to_side(wind_ref, wind_in.at[1 - side], wind_sem, side).start()
+    upper = iota((CX, NY), 0) < 4
+
+    def pack(out, level, first, value):
+        for j in range(NV // 2):
+            one = value[2 * j]
+            two = pltpu.roll(value[2 * j + 1], 4, 0)
+            out[0, level, first + j] = jnp.where(upper, one, two)
+            out[1, level, first + j] = jnp.where(upper, two, one)
+
+    def join(arrived, level, first):
+        tiles = []
+        for j in range(NV // 2):
+            from_left = arrived[0, level, first + j]
+            from_right = arrived[1, level, first + j]
+            tiles.append(jnp.where(upper, from_right, from_left))
+            tiles.append(pltpu.roll(jnp.where(upper, from_left, from_right), 4, 0))
+        return tiles
+
+    def exchange(out, arrived, sems, level):
+        for side in range(2):
+            to_side(
+                out.at[side, level], arrived.at[1 - side, level], sems, side, level
+            ).start()
+
+    def await_sides(arrived, sems, level):
+        for slot in range(2):
+            wait_side(arrived.at[slot, level], sems, slot, level)
+
+    def send_forcing(l):
+        for i in range(3):
+            pack(force_out, l, 2 * i, [forcing_ref[i, v, l] for v in range(NV)])
+        exchange(force_out, force_in, force_sem, l)
 
     edge = jnp.zeros((NV, EXT, NY), F32)
-    for u in (u0, u1, u2, u3):
+    for u in (u0, u1, u2, u3, v0, v1, v2, v3):
         u[0] = edge
         u[LEV + 1] = edge
 
@@ -410,127 +619,95 @@
     def _():
         hop_x[...] = jnp.zeros_like(hop_x)
 
-    for slot in range(2):
-        wait_side(wind_in.at[slot], wind_sem, slot)
-
-    column = iota((EXT, NY), 0)
-    lane = iota((EXT, NY), 1)
-    low_x = jnp.where(first_strip, 4, 0)
-    high_x = jnp.where(last_strip, 11, 15)
-    inside = (column >= low_x) & (column <= high_x)
-    west_ok = inside & ((column > 4) | jnp.logical_not(first_strip))
-    east_ok = inside & ((column < 11) | jnp.logical_not(last_strip))
-    south_ok = inside & (lane > 0)
-    north_ok = inside & (lane < NY - 1)
-
-    def coef_body(l, carry):
-        winds = []
-        for i in range(2):
-            winds.append(
-                jnp.concatenate(
-                    [wind_in[0, i, l, 4:8], wind_ref[i, l], wind_in[1, i, l, 0:4]], axis=0
-                )
-            )
-        wx, wy = winds
-        coef[0, l] = jnp.where(
-            inside, 1.0 - jnp.abs(wx) - jnp.abs(wy) - 4.0 * diffusion - 2.0 * vertical, 0.0
-        )
-        coef[1, l] = jnp.where(west_ok, jnp.maximum(wx, 0.0) + diffusion, 0.0)
-        coef[2, l] = jnp.where(east_ok, jnp.maximum(-wx, 0.0) + diffusion, 0.0)
-        coef[3, l] = jnp.where(south_ok, jnp.maximum(wy, 0.0) + diffusion, 0.0)
-        coef[4, l] = jnp.where(north_ok, jnp.maximum(-wy, 0.0) + diffusion, 0.0)
-        return carry
-
-    lax.fori_loop(0, LEV, coef_body, 0)
-
+    @pl.when(jnp.logical_not(last_group))
+    def _():
+        def early(l, carry):
+            send_forcing(l)
+            return carry
+
+        lax.fori_loop(0, LEV, early, 0)
+
+    inside = inside_grid(first_strip, last_strip)
     mix = [[coupling_step * coupling_ref[v, w] for w in range(NV)] for v in range(NV)]
 
-    def adjoint_level(u, l):
+    def adjoint_level(u, l, rows):
         c, w, e, s, n = [coef[i, l] for i in range(5)]
         now = [u[l + 1, v] for v in range(NV)]
         out = []
         for v in range(NV):
             a = now[v]
-            res = c * a + pltpu.roll(w * a, EXT - 1, 0) + pltpu.roll(e * a, 1, 0)
-            res = res + pltpu.roll(s * a, NY - 1, 1) + pltpu.roll(n * a, 1, 1)
-            res = res + vertical * (u[l, v] + u[l + 2, v])
+            res = c[:rows] * a[:rows]
+            res = res + pltpu.roll(w * a, EXT - 1, 0)[:rows] + pltpu.roll(e * a, 1, 0)[:rows]
+            res = res + ahead(s[:rows] * a[:rows]) + back(n[:rows] * a[:rows])
+            res = res + vertical * (u[l, v, :rows] + u[l + 2, v, :rows])
             for k in range(NV):
-                res = res + mix[k][v] * now[k]
+                res = res + mix[k][v] * now[k][:rows]
             out.append(res)
         return out
 
-    def forward_level(u, l):
-        c, w, e, s, n = [coef[i, l] for i in range(5)]
+    def forward_level(u, l, rows):
+        c, w, e, s, n = [coef[i, l][:rows] for i in range(5)]
         now = [u[l + 1, v] for v in range(NV)]
         out = []
         for v in range(NV):
             a = now[v]
-            res = c * a + w * pltpu.roll(a, 1, 0) + e * pltpu.roll(a, EXT - 1, 0)
-            res = res + s * pltpu.roll(a, 1, 1) + n * pltpu.roll(a, NY - 1, 1)
-            res = res + vertical * (u[l, v] + u[l + 2, v])
+            res = c * a[:rows]
+            res = res + w * pltpu.roll(a, 1, 0)[:rows] + e * pltpu.roll(a, EXT - 1, 0)[:rows]
+            res = res + s * back(a[:rows]) + n * ahead(a[:rows])
+            res = res + vertical * (u[l, v, :rows] + u[l + 2, v, :rows])
             for k in range(NV):
-                res = res + mix[v][k] * now[k]
+                res = res + mix[v][k] * now[k][:rows]
             out.append(res)
         return out
 
     def in_range(l):
         return (l >= 0) & (l < LEV)
 
-    def adjoint_tick(k, carry):
-        @pl.when(k < LEV)
+    def adjoint_tick(k):
+        @pl.when(in_range(k))
         def _():
             @pl.when(jnp.logical_not(last_group))
             def _():
                 hop(hop_a, hop_a, 0, k, later).wait_recv()
 
             value = [hop_a[k, v] + forcing_ref[3, v, k] for v in range(NV)]
+            pack(adj_out, k, 0, value)
+            exchange(adj_out, adj_in, adj_sem, k)
+
+            @pl.when(last_group)
+            def _():
+                send_forcing(k)
+
             for v in range(NV):
-                u0[k + 1, v, 4 : 4 + CX] = value[v]
-            for side in range(2):
-                lo = 4 * side
-                buf = halo_out.at[side, k]
-                pack_four(buf.at[0:2], value, lo)
-                pack_four(buf.at[2:4], [forcing_ref[2, v, k] for v in range(NV)], lo)
-                lo = 6 * side
-                pack_two(buf.at[4], [forcing_ref[1, v, k] for v in range(NV)], lo)
-                pack_two(buf.at[5], [forcing_ref[0, v, k] for v in range(NV)], lo)
-                to_side(buf, halo_in.at[1 - side, k], halo_sem, side, k).start()
-
-        m = k - DELAY
+                u0[k + 1, v, :CX] = value[v]
+
+        m = k - ADJ_DELAY
 
         @pl.when(in_range(m))
         def _():
-            for slot in range(2):
-                wait_side(halo_in.at[slot, m], halo_sem, slot, m)
-            for v in range(NV):
-                rows = slice((v % 2) * 4, (v % 2) * 4 + 4)
-                pair = slice(2 * v, 2 * v + 2)
-                u0[m + 1, v, 0:4] = halo_in[0, m, v // 2, rows]
-                u0[m + 1, v, 12:16] = halo_in[1, m, v // 2, rows]
-                fext[2, m, v, 0:4] = halo_in[0, m, 2 + v // 2, rows]
-                fext[2, m, v, 12:16] = halo_in[1, m, 2 + v // 2, rows]
-                fext[2, m, v, 4:12] = forcing_ref[2, v, m]
-                for i, tile in ((1, 4), (0, 5)):
-                    fext[i, m, v, 0:2] = jnp.zeros((2, NY), F32)
-                    fext[i, m, v, 14:16] = jnp.zeros((2, NY), F32)
-                    fext[i, m, v, 2:4] = halo_in[0, m, tile, pair]
-                    fext[i, m, v, 12:14] = halo_in[1, m, tile, pair]
-                    fext[i, m, v, 4:12] = forcing_ref[i, v, m]
+            await_sides(adj_in, adj_sem, m)
+            await_sides(force_in, force_sem, m)
+            for v, tile in enumerate(join(adj_in, m, 0)):
+                u0[m + 1, v, CX:] = tile
+            for i in range(3):
+                for v, tile in enumerate(join(force_in, m, 2 * i)):
+                    fext[i, m, v] = tile
 
         for i, (src, dst) in enumerate(((u0, u1), (u1, u2), (u2, u3))):
             level = m - 1 - i
 
             @pl.when(in_range(level))
             def _():
-                res = adjoint_level(src, level)
+                res = adjoint_level(src, level, EXT)
                 for v in range(NV):
-                    dst[level + 1, v] = res[v] + fext[2 - i, level, v]
+                    dst[level + 1, v, :CX] = res[v][:CX] + forcing_ref[2 - i, v, level]
+                    dst[level + 1, v, CX:] = res[v][CX:] + fext[2 - i, level, v]
 
         level = m - 4
 
         @pl.when(in_range(level))
         def _():
-            res = [r[4 : 4 + CX] for r in adjoint_level(u3, level)]
+            res = adjoint_level(u3, level, CX)
             for v in range(NV):
                 fin_a[level, v] = res[v]
 
@@ -538,85 +715,66 @@
             def _():
                 hop(fin_a, hop_a, 0, level, earlier).start()
 
-            for side in range(2):
-                pack_two(cov_out.at[side, level], res, 6 * side)
-                to_side(
-                    cov_out.at[side, level], cov_in.at[1 - side, level], cov_sem, side, level
-                ).start()
-
-        return carry
-
-    lax.fori_loop(0, LEV + DELAY + 4, adjoint_tick, 0)
+            pack(cov_out, level, 0, res)
+            exchange(cov_out, cov_in, cov_sem, level)
 
     lane_low = jnp.where(iota((CX, NY), 1) > 0, 1.0, 0.0)
     lane_high = jnp.where(iota((CX, NY), 1) < NY - 1, 1.0, 0.0)
     keep = jnp.where(inside, 1.0, 0.0)
 
-    def cov_level(l, carry):
-        for slot in range(2):
-            wait_side(cov_in.at[slot, l], cov_sem, slot, l)
-        zero = jnp.zeros((2, NY), F32)
-        for v in range(NV):
-            pair = slice(2 * v, 2 * v + 2)
-            scale = scale_ref[v, l]
-            ext = jnp.concatenate(
-                [zero, cov_in[0, l, pair], fin_a[l, v], cov_in[1, l, pair], zero], axis=0
-            )
-            ext = ext * (keep * scale)
-            ext = 0.5 * ext + 0.25 * (pltpu.roll(ext, 1, 0) + pltpu.roll(ext, EXT - 1, 0))
-            ext = ext * keep
-            ext = 0.5 * ext + 0.25 * (pltpu.roll(ext, 1, 0) + pltpu.roll(ext, EXT - 1, 0))
-            own = ext[4 : 4 + CX]
-            for _ in range(2):
-                own = 0.5 * own + 0.25 * (
-                    lane_low * pltpu.roll(own, 1, 1) + lane_high * pltpu.roll(own, NY - 1, 1)
-                )
-            inc[l, v] = own * scale
-        return carry
-
-    lax.fori_loop(0, LEV, cov_level, 0)
-
-    def forward_tick(k, carry):
-        @pl.when(k < LEV)
+    def cov_tick(l):
+        @pl.when(in_range(l))
+        def _():
+            await_sides(cov_in, cov_sem, l)
+            for v, tile in enumerate(join(cov_in, l, 0)):
+                scale = scale_ref[v, l]
+                ext = jnp.concatenate([fin_a[l, v], tile], axis=0) * (keep * scale)
+                ext = 0.5 * ext + 0.25 * (pltpu.roll(ext, 1, 0) + pltpu.roll(ext, EXT - 1, 0))
+                ext = ext * keep
+                ext = 0.5 * ext + 0.25 * (pltpu.roll(ext, 1, 0) + pltpu.roll(ext, EXT - 1, 0))
+                own = ext[:CX]
+                for _ in range(2):
+                    own = 0.5 * own + 0.25 * (lane_low * back(own) + lane_high * ahead(own))
+                inc[l, v] = own * scale
+
+    fwd_delay = jnp.where(first_group, FIRST_DELAY, FWD_DELAY)
+
+    def forward_tick(k):
+        @pl.when(in_range(k))
         def _():
             @pl.when(jnp.logical_not(first_group))
             def _():
                 hop(hop_x, hop_x, 1, k, earlier).wait_recv()
 
             value = [hop_x[k, v] + inc[k, v] for v in range(NV)]
+            pack(fwd_out, k, 0, value)
+            exchange(fwd_out, fwd_in, fwd_sem, k)
             for v in range(NV):
-                u0[k + 1, v, 4 : 4 + CX] = value[v]
-            for side in range(2):
-                buf = fwd_out.at[side, k]
-                pack_four(buf, value, 4 * side)
-                to_side(buf, fwd_in.at[1 - side, k], fwd_sem, side, k).start()
-
-        m = k - DELAY
+                v0[k + 1, v, :CX] = value[v]
+
+        m = k - fwd_delay
 
         @pl.when(in_range(m))
         def _():
-            for slot in range(2):
-                wait_side(fwd_in.at[slot, m], fwd_sem, slot, m)
-            for v in range(NV):
-                rows = slice((v % 2) * 4, (v % 2) * 4 + 4)
-                u0[m + 1, v, 0:4] = fwd_in[0, m, v // 2, rows]
-                u0[m + 1, v, 12:16] = fwd_in[1, m, v // 2, rows]
-
-        for i, (src, dst) in enumerate(((u0, u1), (u1, u2), (u2, u3))):
+            await_sides(fwd_in, fwd_sem, m)
+            for v, tile in enumerate(join(fwd_in, m, 0)):
+                v0[m + 1, v, CX:] = tile
+
+        for i, (src, dst) in enumerate(((v0, v1), (v1, v2), (v2, v3))):
             level = m - 1 - i
 
             @pl.when(in_range(level))
             def _():
-                res = forward_level(src, level)
+                res = forward_level(src, level, EXT)
                 for v in range(NV):
                     dst[level + 1, v] = res[v]
-                    state_ref[i, v, level] = res[v][4 : 4 + CX]
+                    state_ref[i, v, level] = res[v][:CX]
 
         level = m - 4
 
         @pl.when(in_range(level))
         def _():
-            res = [r[4 : 4 + CX] for r in forward_level(u3, level)]
+            res = forward_level(v3, level, CX)
             for v in range(NV):
                 state_ref[3, v, level] = res[v]
                 fin_x[level, v] = res[v]
@@ -625,18 +783,28 @@
             def _():
                 hop(fin_x, hop_x, 1, level, later).start()
 
+    adjoint_ticks = LEV + ADJ_DELAY + 4
+    behind = jnp.where(first_group, ADJ_DELAY + 4 + COV_DELAY, adjoint_ticks)
+
+    def tick(k, carry):
+        adjoint_tick(k)
+        cov_tick(k - (ADJ_DELAY + 4 + COV_DELAY))
+        forward_tick(k - behind)
         return carry
 
-    lax.fori_loop(0, LEV + DELAY + 4, forward_tick, 0)
-
-    for side in range(2):
-        to_side(wind_ref, wind_in.at[1 - side], wind_sem, side).wait_send()
+    lax.fori_loop(0, behind + LEV + fwd_delay + 4, tick, 0)
 
     def drain(l, carry):
-        for side in range(2):
-            to_side(halo_out.at[side, l], halo_in.at[1 - side, l], halo_sem, side, l).wait_send()
-            to_side(cov_out.at[side, l], cov_in.at[1 - side, l], cov_sem, side, l).wait_send()
-            to_side(fwd_out.at[side, l], fwd_in.at[1 - side, l], fwd_sem, side, l).wait_send()
+        for out, arrived, sems in (
+            (adj_out, adj_in, adj_sem),
+            (force_out, force_in, force_sem),
+            (cov_out, cov_in, cov_sem),
+            (fwd_out, fwd_in, fwd_sem),
+        ):
+            for side in range(2):
+                to_side(
+                    out.at[side, l], arrived.at[1 - side, l], sems, side, l
+                ).wait_send()
 
         @pl.when(jnp.logical_not(first_group))
         def _():
@@ -651,43 +819,28 @@
     lax.fori_loop(0, LEV, drain, 0)
 
 
-def sweeps(forcing, winds, coupling, scale):
-    state = (LEV, NV, CX, NY)
-    padded = (LEV + 2, NV, EXT, NY)
-    dma = pltpu.SemaphoreType.DMA
+def sweeps(forcing, coef, coupling, scale):
+    state = pltpu.VMEM((LEV, NV, CX, NY), F32)
+    padded = pltpu.VMEM((LEV + 2, NV, EXT, NY), F32)
+    edges = pltpu.VMEM((2, LEV, 2, CX, NY), F32)
+    wide_edges = pltpu.VMEM((2, LEV, 6, CX, NY), F32)
+    levels = pltpu.SemaphoreType.DMA((2, 2, LEV))
     return pl.pallas_call(
         sweep_kernel,
         out_shape=jax.ShapeDtypeStruct((STEPS, NV, LEV, CX, NY), F32),
         in_specs=[VMEM, VMEM, SMEM, SMEM],
         out_specs=VMEM,
-        scratch_shapes=[
-            pltpu.VMEM((2, 2, LEV, CX, NY), F32),
-            pltpu.VMEM((5, LEV, EXT, NY), F32),
-            pltpu.VMEM(state, F32),
-            pltpu.VMEM(state, F32),
-            pltpu.VMEM(state, F32),
-            pltpu.VMEM(state, F32),
-            pltpu.VMEM((2, LEV, 6, 8, NY), F32),
-            pltpu.VMEM((2, LEV, 6, 8, NY), F32),
-            pltpu.VMEM((2, LEV, 8, NY), F32),
-            pltpu.VMEM((2, LEV, 8, NY), F32),
-            pltpu.VMEM((2, LEV, 2, 8, NY), F32),
-            pltpu.VMEM((2, LEV, 2, 8, NY), F32),
-            pltpu.VMEM((3, LEV, NV, EXT, NY), F32),
-            pltpu.VMEM(padded, F32),
-            pltpu.VMEM(padded, F32),
-            pltpu.VMEM(padded, F32),
-            pltpu.VMEM(padded, F32),
-            pltpu.VMEM(state, F32),
-            dma((2, 2)),
-            dma((2, 2, LEV)),
-            dma((2, 2, LEV)),
-            dma((2, 2, LEV)),
-            dma((2, 2, LEV)),
-        ],
-        compiler_params=params(48, collective_id=1, has_side_effects=True),
+        scratch_shapes=[state] * 4
+        + [edges] * 2
+        + [wide_edges] * 2
+        + [edges] * 4
+        + [pltpu.VMEM((3, LEV, NV, CX, NY), F32)]
+        + [padded] * 8
+        + [state]
+        + [levels] * 5,
+        compiler_params=params(34, collective_id=1, has_side_effects=True),
         name="sweeps",
-    )(forcing, winds, coupling, scale)
+    )(forcing, coef, coupling, scale)
 
 
 def per_device(
@@ -717,19 +870,30 @@
         ],
         axis=0,
     )
-    outgoing, rank = pl.pallas_call(
-        pack_kernel,
+    winds = jnp.concatenate([wind_x, wind_y], axis=0)
+    tiles = pltpu.VMEM((devices, 8, CAP), F32)
+    arrived, rank, coef = pl.pallas_call(
+        route_kernel,
         out_shape=(
             jax.ShapeDtypeStruct((devices, 8, CAP), F32),
             jax.ShapeDtypeStruct((1, rows), jnp.int32),
+            jax.ShapeDtypeStruct((5, LEV, EXT, NY), F32),
         ),
-        in_specs=[VMEM, VMEM],
-        out_specs=(VMEM, VMEM),
-        scratch_shapes=[pltpu.VMEM((devices, sum(PACK_PARTS) * CAP), F32)],
-        compiler_params=params(48),
-        name="pack",
-    )(route, fields)
-    arrived = lax.all_to_all(outgoing, ("tm", "space"), split_axis=0, concat_axis=0, tiled=True)
+        in_specs=[VMEM, VMEM, VMEM],
+        out_specs=(VMEM, VMEM, VMEM),
+        scratch_shapes=[
+            tiles,
+            tiles,
+            pltpu.VMEM((devices, sum(PACK_PARTS) * CAP), F32),
+            pltpu.VMEM((2, LEV, CX, NY), F32),
+            pltpu.VMEM((2, 2, LEV, CX, NY), F32),
+            pltpu.SemaphoreType.DMA,
+            pltpu.SemaphoreType.DMA,
+            pltpu.SemaphoreType.DMA((2, 2)),
+        ],
+        compiler_params=params(20, collective_id=2, has_side_effects=True),
+        name="route",
+    )(route, fields, winds)
     slots = devices * CAP
     forcing, ordered, position, starts = pl.pallas_call(
         sort_scatter_kernel,
@@ -745,20 +909,17 @@
             pltpu.VMEM((slots // CHUNK, CHUNK), F32),
             pltpu.VMEM((SORT_ROWS, SORT_PARTS * CAP), F32),
         ],
-        compiler_params=params(48),
+        compiler_params=params(20),
         name="sort_scatter",
     )(arrived)
-    winds = jnp.concatenate([wind_x, wind_y], axis=0)
-    states = sweeps(
-        forcing.reshape(STEPS, NV, LEV, CX, NY), winds, coupling, cov_scale[0]
-    )
+    states = sweeps(forcing.reshape(STEPS, NV, LEV, CX, NY), coef, coupling, cov_scale[0])
     returning = pl.pallas_call(
         gather_kernel,
         out_shape=jax.ShapeDtypeStruct((devices, 2 * CAP), F32),
         in_specs=[SMEM, VMEM, VMEM, VMEM, VMEM, VMEM],
         out_specs=VMEM,
         scratch_shapes=[pltpu.VMEM((256, CAP), F32)],
-        compiler_params=params(48),
+        compiler_params=params(20),
         name="gather",
     )(
         starts,
@@ -768,17 +929,21 @@
         arrived,
         residual_dual.reshape(wide),
     )
-    back = lax.all_to_all(returning, ("tm", "space"), split_axis=0, concat_axis=0, tiled=True)
     out = jax.ShapeDtypeStruct(wide, F32)
     results = pl.pallas_call(
         final_kernel,
         out_shape=(out, out, out),
         in_specs=[VMEM] * 6,
         out_specs=(VMEM, VMEM, VMEM),
-        compiler_params=params(48),
+        scratch_shapes=[
+            pltpu.VMEM((devices, 1, 2 * CAP), F32),
+            pltpu.SemaphoreType.DMA,
+            pltpu.SemaphoreType.DMA,
+        ],
+        compiler_params=params(12, collective_id=3, has_side_effects=True),
         name="final",
     )(
-        back,
+        returning.reshape(devices, 1, 2 * CAP),
         route.reshape(wide),
         rank.reshape(wide),
         dual_weights.reshape(wide),

time: 270 us -> 227 us (0.84)
  starting transfers between devices: 64.5 us -> 0 us
  Pallas kernels: 176 us -> 219 us
  waiting for transfers between devices: 20.5 us -> 0 us
    all_to_all x2 -> x0, starting transfers between devices: 64.5 us -> none  [the longest x1 53 us: per_device(): lax.all_to_all(returning, ('tm', 'space'), split_axis=0, concat_axis=0, t...]
    pallas_call x1, Pallas kernels: 1.55 us -> 53.6 us  [per_device(): pl.pallas_call(final_kernel, out_shape=(out, out, out), in_specs=[VMEM] *...]
    pallas_call x1, Pallas kernels: 108 us -> 80.5 us  [sweeps(): pl.pallas_call(sweep_kernel, out_shape=jax.ShapeDtypeStruct((STEPS, NV, L...]
    all_to_all x2 -> x0, waiting for transfers between devices: 20.5 us -> none  [the longest x1 12.9 us: per_device(): lax.all_to_all(outgoing, ('tm', 'space'), split_axis=0, concat_axis=0, ti...]
    pallas_call x1, Pallas kernels: 15.9 us -> 32.3 us  [per_device(): pl.pallas_call(route_kernel, out_shape=(jax.ShapeDtypeStruct((devices, 8,...]
  transfers between devices with their start and end apart: 2 -> 0, of which waited for: 2 -> 0; matrix products, arithmetic and copies ran while one was open for 1% -> 0% of each run, Pallas kernels for 0% -> 0%
where the time goes in v2:
time: 227 us
  Pallas kernels  219 us (96%)
  local copies, waits for them, and re-layouts  3.88 us (2%)
  other arithmetic  3.2 us (1%)
    pallas_call x1, Pallas kernels, sweeps(): pl.pallas_call(sweep_kernel, out_shape=jax.ShapeDtypeStruct((STEPS, NV, L...  80.5 us
    pallas_call x1, Pallas kernels, per_device(): pl.pallas_call(final_kernel, out_shape=(out, out, out), in_specs=[VMEM] *...  53.6 us
    pallas_call x1, Pallas kernels, per_device(): pl.pallas_call(sort_scatter_kernel, out_shape=(jax.ShapeDtypeStruct((BUCK...  35 us
    pallas_call x1, Pallas kernels, per_device(): pl.pallas_call(route_kernel, out_shape=(jax.ShapeDtypeStruct((devices, 8,...  32.3 us
    pallas_call x1, Pallas kernels, per_device(): pl.pallas_call(gather_kernel, out_shape=jax.ShapeDtypeStruct((devices, 2...  17.8 us

profile of v2, /device:TPU:1, one launch (start us, length us, event | category | flops | bytes accessed | tf_op | source)
XLA Modules:
  0.0 227.1 jit_solution(17383836443036746683)
XLA Ops:
  0.6 0.0 copy-start.3
  0.6 0.0 copy-start.2
  0.7 0.8 add_convert_fusion
  1.4 1.2 concatenate.6.field_ref
  2.6 1.0 pad_maximum_fusion.wind_ref
  3.6 0.0 copy-start
  3.6 0.7 copy-done
  4.3 32.3 %route.1 = (f32[128,8,128]{2,1,0:T(8,128)S(1)}, s32[1,8192]{1,0:T(1,128)S(1)}, f32[5,16,16,256]{3,2,1,0:T(8,128)S(1)}) custom-call(s32[1,8192]{1,0:T(1,128)S(1)} %bitcast.21, f32[8,8192]{1,0:T(8,128)S(1)} %concatenate.6.field_ref, f32[2,16,8,256]{3,2,1,0:T(8,128)S(1)} %pad_maximum_fusion.wind_ref), custom_call_target="tpu_custom_call" | custom-call | tf_op jit(solution)/shard_map/route/pallas_call | solution.py:875
  36.6 35.0 %sort_scatter.1 = (f32[16,128,256]{2,1,0:T(8,128)S(1)}, f32[6,160,128]{2,1,0:T(8,128)S(1)}, s32[16,1024]{1,0:T(8,128)S(1)}, s32[1,17]{1,0:T(1,128)S(1)}) custom-call(f32[128,8,128]{2,1,0:T(8,128)S(1)} %get-tuple-element.13.recv_ref), custom_call_target="tpu_custom_call" | custom-call | tf_op jit(solution)/shard_map/sort_scatter/pallas_call | solution.py:898
  71.6 0.0 copy-done.3
  71.6 0.0 copy-start.4
  71.6 80.5 %sweeps.1 = f32[4,4,16,8,256]{4,3,2,1,0:T(8,128)S(1)} custom-call(f32[4,4,16,8,256]{4,3,2,1,0:T(8,128)S(1)} %bitcast.20, f32[5,16,16,256]{3,2,1,0:T(8,128)S(1)} %get-tuple-element.16.coef, f32[4,4]{1,0:T(4,128)S(1)} %copy-done.2, f32[4,16]{1,0:T(4,128)S(1)} %bitcast.25), custom_call_target="tpu_custom_call" | custom-call | tf_op jit(solution)/shard_map/sweeps/pallas_call | solution.py:828
  152.2 0.0 copy-start.1
  152.2 0.0 copy-start.6
  152.2 0.0 copy-start.5
  152.2 0.0 copy-done.4
  152.2 17.8 %gather.1 = f32[128,256]{1,0:T(8,128)S(1)} custom-call(s32[1,17]{1,0:T(1,128)S(1)} %get-tuple-element.14.start_ref, f32[16,128,256]{2,1,0:T(8,128)S(1)} %bitcast.19, f32[6,160,128]{2,1,0:T(8,128)S(1)} %get-tuple-element.17.sorted_ref, s32[16,1024]{1,0:T(8,128)S(1)} %get-tuple-element.18.pos_ref, f32[128,8,128]{2,1,0:T(8,128)S(1)} %get-tuple-element.13.recv_ref, ...), custom_call_target="tpu_custom_call" | custom-call | tf_op jit(solution)/shard_map/gather/pallas_call | solution.py:916
  170.0 0.1 reshape.44.out_ref
  170.1 0.5 broadcast.6
  170.7 0.7 reduce.7
  171.4 0.7 reduce.6
  172.2 53.6 %final.1 = (f32[8,1024]{1,0:T(8,128)S(1)}, f32[8,1024]{1,0:T(8,128)S(1)}, f32[8,1024]{1,0:T(8,128)S(1)}) custom-call(f32[128,1,256]{2,1,0:T(1,128)S(1)} %reshape.44.out_ref, s32[8,1024]{1,0:T(8,128)S(1)} %reshape_reshape.3.route_ref, s32[8,1024]{1,0:T(8,128)S(1)} %reshape.45.rank_ref, f32[8,1024]{1,0:T(8,128)S(1)} %reshape.46.dual_ref, ...), custom_call_target="tpu_custom_call" | custom-call | tf_op jit(solution)/shard_map/final/pallas_call | solution.py:933
  225.8 0.6 copy_bitcast_fusion
  226.5 0.6 copy.20
  (9 shorter events, 0.1 us)
Async XLA Ops:
  0.6 71.0 %copy-start.3 = (f32[1,4,16]{2,1,0:T(4,128)S(1)}, f32[1,4,16]{2,1,0:T(4,128)}, u32[]{:S(2)}) copy-start(f32[1,4,16]{2,1,0:T(4,128)} %param.21) | copy-start | bytes 772
  0.6 71.0 %copy-start.2 = (f32[4,4]{1,0:T(4,128)S(1)}, f32[4,4]{1,0:T(4,128)}, u32[]{:S(2)}) copy-start(f32[4,4]{1,0:T(4,128)} %coupling_ref.1) | copy-start | bytes 196
  3.6 0.8 copy-start
  71.6 80.6 %copy-start.4 = (f32[8192]{0:T(1024)S(1)}, f32[8192]{0:T(1024)}, u32[]{:S(2)}) copy-start(f32[8192]{0:T(1024)} %param.13) | copy-start | bytes 98308
  152.2 19.2 %copy-start.1 = (s32[8192,1]{0,1:T(1,128)S(1)}, s32[8192,1]{0,1:T(1,128)}, u32[]{:S(2)}) copy-start(s32[8192,1]{0,1:T(1,128)} %param.15) | copy-start | bytes 98308
  152.2 20.0 %copy-start.6 = (f32[8192]{0:T(1024)S(1)}, f32[8192]{0:T(1024)}, u32[]{:S(2)}) copy-start(f32[8192]{0:T(1024)} %param.11) | copy-start | bytes 98308
  152.2 20.0 %copy-start.5 = (f32[8192]{0:T(1024)S(1)}, f32[8192]{0:T(1024)}, u32[]{:S(2)}) copy-start(f32[8192]{0:T(1024)} %param.12) | copy-start | bytes 98308

commit v3 on v2

--- a/solution.py
+++ b/solution.py
@@ -20,10 +20,10 @@
 SUB = 256
 HALF = NY // 2
 EXT = 2 * CX
-ADJ_DELAY = 5
-COV_DELAY = 5
-FWD_DELAY = 5
-FIRST_DELAY = 5
+ADJ_DELAY = 4
+COV_DELAY = 4
+FWD_DELAY = 4
+FIRST_DELAY = 4
 diffusion = 0.05
 vertical = 0.05
 coupling_step = 0.05
@@ -32,6 +32,7 @@
 BF16 = jnp.bfloat16
 VMEM = pl.BlockSpec(memory_space=pltpu.VMEM)
 SMEM = pl.BlockSpec(memory_space=pltpu.SMEM)
+ANY = pl.BlockSpec(memory_space=pltpu.HBM)
 
 
 def params(mib, **kw):
@@ -62,6 +63,11 @@
 
 def one_hot(mask):
     return jnp.where(mask, 1.0, 0.0).astype(BF16)
+
+
+def short_hot(ids, row):
+    same = ids.astype(jnp.int16) == row.astype(jnp.int16)
+    return jnp.where(same, jnp.ones((), BF16), jnp.zeros((), BF16))
 
 
 def running_rank(hot, hot_mask, carry, upper):
@@ -86,34 +92,53 @@
     return one_hot(iota((SUB, SUB), 0) < iota((SUB, SUB), 1))
 
 
-PACK_PARTS = (3, 2, 2, 2, 2, 2, 2, 2)
-
-
-def everyone(me, act):
+PACK_PARTS = (3, 2, 2, 2, 2, 2, 2)
+
+
+ROW_STRIPS = 8
+
+
+def backwards(within):
+    return ROW_STRIPS - 2 - within + 2 * (within % 2)
+
+
+def strip_of(t):
+    row = t // ROW_STRIPS
+    within = t % ROW_STRIPS
+    return row * ROW_STRIPS + jnp.where(row % 2 == 1, backwards(within), within)
+
+
+def around(start, step, size):
+    index = start + step
+    return jnp.where(index >= size, index - size, index)
+
+
+def everyone(act):
     g = lax.axis_index("tm")
     t = lax.axis_index("space")
     groups = lax.axis_size("tm")
-    strips = lax.axis_size("space")
-    for step in range(groups):
-        group = g + step
-        group = jnp.where(group >= groups, group - groups, group)
-
-        def body(i, carry):
-            strip = t + i
-            strip = jnp.where(strip >= strips, strip - strips, strip)
-            act(group * strips + strip, (group, strip))
-            return carry
-
-        lax.fori_loop(0 if step else 1, strips, body, 0, unroll=True)
-
-
-def greet_all(me):
+    rows = lax.axis_size("space") // ROW_STRIPS
+    ways = []
+    for step in range(ROW_STRIPS):
+        within = around(t % ROW_STRIPS, step, ROW_STRIPS)
+        ways.append((within, backwards(within)))
+    for group_step in range(groups):
+        group = around(g, group_step, groups)
+        for row_step in range(rows):
+            row = around(t // ROW_STRIPS, row_step, rows)
+            first = row * ROW_STRIPS
+            odd = row % 2 == 1
+            for step, (within, turned) in enumerate(ways):
+                if group_step or row_step or step:
+                    act(group, first + within, first + jnp.where(odd, turned, within))
+
+
+def greet_all():
     barrier = pltpu.get_barrier_semaphore()
     everyone(
-        me,
-        lambda peer, device: pl.semaphore_signal(
-            barrier, inc=1, device_id=device, device_id_type=MESH
-        ),
+        lambda group, place, strip: pl.semaphore_signal(
+            barrier, inc=1, device_id=(group, place), device_id_type=MESH
+        )
     )
 
 
@@ -123,18 +148,21 @@
 
 
 def send_all(me, out, arrived, send_sem, recv_sem):
-    def start(peer, device):
+    strips = lax.axis_size("space")
+
+    def start(group, place, strip):
         pltpu.make_async_remote_copy(
-            src_ref=out.at[peer],
+            src_ref=out.at[group * strips + strip],
             dst_ref=arrived.at[me],
             send_sem=send_sem,
             recv_sem=recv_sem,
-            device_id=device,
+            device_id=(group, place),
             device_id_type=MESH,
         ).start()
 
-    pltpu.make_async_copy(out.at[me], arrived.at[me], recv_sem).start()
-    everyone(me, start)
+    own = lax.axis_index("tm") * strips + strip_of(lax.axis_index("space"))
+    pltpu.make_async_copy(out.at[own], arrived.at[me], recv_sem).start()
+    everyone(start)
 
 
 def receive_all(arrived, recv_sem):
@@ -151,9 +179,14 @@
 
 
 def route_kernel(
-    route_ref,
-    field_ref,
-    wind_ref,
+    route_hbm,
+    cell_hbm,
+    interp_hbm,
+    d_hbm,
+    r_hbm,
+    var_hbm,
+    wind_x_hbm,
+    wind_y_hbm,
     arrived_ref,
     rank_ref,
     coef,
@@ -162,26 +195,54 @@
     acc_ref,
     wind_own,
     wind_in,
+    route_ref,
+    cell_ref,
+    interp_ref,
+    d_ref,
+    r_ref,
+    var_ref,
+    wind_x_ref,
+    wind_y_ref,
     send_sem,
     recv_sem,
     wind_sem,
+    fetch_sem,
 ):
+    fetches = [
+        pltpu.make_async_copy(src, dst, fetch_sem.at[i])
+        for i, (src, dst) in enumerate(
+            (
+                (wind_x_hbm, wind_x_ref),
+                (wind_y_hbm, wind_y_ref),
+                (route_hbm, route_ref),
+                (cell_hbm, cell_ref),
+                (interp_hbm, interp_ref),
+                (d_hbm, d_ref),
+                (r_hbm, r_ref),
+                (var_hbm, var_ref),
+            )
+        )
+    ]
+    for fetch in fetches:
+        fetch.start()
     me = my_index()
     g = lax.axis_index("tm")
     t = lax.axis_index("space")
     strips = lax.axis_size("space")
-    sides = ((g, lax.rem(t + strips - 1, strips)), (g, lax.rem(t + 1, strips)))
-    first_strip = t == 0
-    last_strip = t == strips - 1
-    greet_all(me)
+    strip = strip_of(t)
+    stays = strip == t
+    first_strip = strip == 0
+    last_strip = strip == strips - 1
+    greet_all()
+    for fetch in fetches:
+        fetch.wait()
 
     order = iota((NY, NY), 1)
     order = one_hot(iota((NY, NY), 0) == (order % HALF) * 2 + order // HALF)
-    rows = 2 * LEV * CX
-    turned = parts_of(wind_ref[...].reshape(rows, NY), 3)
-    wind_own[...] = (nn(turned[0], order) + nn(turned[1], order) + nn(turned[2], order)).reshape(
-        2, LEV, CX, NY
-    )
+    for i, wind in enumerate((wind_x_ref, wind_y_ref)):
+        turned = parts_of(wind[...].reshape(LEV * CX, NY), 3)
+        turned = nn(turned[0], order) + nn(turned[1], order) + nn(turned[2], order)
+        wind_own[i] = turned.reshape(LEV, CX, NY)
 
     devices = out_ref.shape[0]
     upper = upper_strict()
@@ -196,15 +257,44 @@
         rank = rank.astype(jnp.int32)
         rank_ref[:, lanes] = rank
         slot = one_hot(iota((CAP, CHUNK), 0) == rank)
-        fields = field_ref[:, lanes]
+        fields = [(cell_ref[:, lanes] + 1).astype(F32)]
+        fields += [interp_ref[f : f + 1, lanes] for f in range(3)]
+        fields += [d_ref[:, lanes], r_ref[:, lanes], var_ref[:, lanes]]
         pieces = []
-        for f, count in enumerate(PACK_PARTS):
-            for part in parts_of(fields[f : f + 1], count):
+        for field, count in zip(fields, PACK_PARTS):
+            for part in parts_of(field, count):
                 pieces.append(slot * part)
         acc_ref[...] += nt(hot, jnp.concatenate(pieces, axis=0))
         return carry
 
-    lax.fori_loop(0, route_ref.shape[1] // CHUNK, body, jnp.zeros((devices, 1), F32))
+    chunks = route_ref.shape[1] // CHUNK
+    carry = jnp.zeros((devices, 1), F32)
+    carry = lax.fori_loop(0, chunks // 2, body, carry, unroll=2)
+    await_all()
+
+    def to_strip(slot):
+        other = lax.rem(t + strips + 1 - slot, strips)
+        return pltpu.make_async_remote_copy(
+            src_ref=wind_own,
+            dst_ref=wind_in.at[slot],
+            send_sem=wind_sem.at[0, slot],
+            recv_sem=wind_sem.at[1, slot],
+            device_id=(g, strip_of(other)),
+            device_id_type=MESH,
+        )
+
+    to_strip(0).start()
+    to_strip(2).start()
+
+    @pl.when(stays)
+    def _():
+        pltpu.make_async_copy(wind_own, wind_in.at[1], wind_sem.at[1, 1]).start()
+
+    @pl.when(jnp.logical_not(stays))
+    def _():
+        to_strip(1).start()
+
+    lax.fori_loop(chunks // 2, chunks, body, carry, unroll=2)
     at = 0
     for f, count in enumerate(PACK_PARTS):
         total = acc_ref[:, at * CAP : (at + 1) * CAP]
@@ -212,24 +302,10 @@
             total = total + acc_ref[:, (at + i) * CAP : (at + i + 1) * CAP]
         at += count
         out_ref[:, f, :] = total
-
-    await_all()
-
-    def to_side(side):
-        return pltpu.make_async_remote_copy(
-            src_ref=wind_own,
-            dst_ref=wind_in.at[1 - side],
-            send_sem=wind_sem.at[0, side],
-            recv_sem=wind_sem.at[1, 1 - side],
-            device_id=sides[side],
-            device_id_type=MESH,
-        )
-
+    out_ref[:, 7, :] = jnp.zeros_like(out_ref[:, 7, :])
     send_all(me, out_ref, landing, send_sem, recv_sem)
-    for side in range(2):
-        to_side(side).start()
-    for side in range(2):
-        to_side(side).wait_recv()
+    for slot in range(3):
+        pltpu.make_async_copy(wind_in.at[slot], wind_in.at[slot], wind_sem.at[1, slot]).wait()
 
     column = iota((EXT, NY), 0)
     lane = iota((EXT, NY), 1)
@@ -245,7 +321,7 @@
     def coef_body(l, carry):
         wx, wy = [
             jnp.concatenate(
-                [wind_own[i, l], jnp.where(from_right, wind_in[1, i, l], wind_in[0, i, l])], axis=0
+                [wind_in[1, i, l], jnp.where(from_right, wind_in[2, i, l], wind_in[0, i, l])], axis=0
             )
             for i in range(2)
         ]
@@ -261,8 +337,13 @@
     lax.fori_loop(0, LEV, coef_body, 0)
     receive_all(landing, recv_sem)
     arrived_ref[...] = landing[...]
-    for side in range(2):
-        to_side(side).wait_send()
+    to_strip(0).wait_send()
+    to_strip(2).wait_send()
+
+    @pl.when(jnp.logical_not(stays))
+    def _():
+        to_strip(1).wait_send()
+
     finish_sends(out_ref, send_sem)
 
 
@@ -279,10 +360,10 @@
     return jnp.concatenate([ref[base + i, field : field + 1, :] for i in range(per)], axis=1)
 
 
-SORT_PARTS = 12
-
-
-def sort_scatter_kernel(recv_ref, forcing_ref, sorted_ref, pos_ref, start_ref, rank_ref, acc_ref):
+SORT_PARTS = 10
+
+
+def sort_scatter_kernel(recv_ref, forcing_ref, sorted_ref, pos_ref, bucket_ref, rank_ref, acc_ref):
     chunks = recv_ref.shape[0] * CAP // CHUNK
     upper = upper_strict()
 
@@ -297,16 +378,21 @@
         rank_ref[pl.ds(c, 1), :] = rank
         return carry
 
-    totals = lax.fori_loop(0, chunks, count_body, jnp.zeros((BUCKETS, 1), F32))
+    totals = lax.fori_loop(0, chunks, count_body, jnp.zeros((BUCKETS, 1), F32), unroll=4)
     tiles = jnp.floor((totals + (SUB - 1.0)) * (1.0 / SUB))
     before = jnp.zeros((BUCKETS, 1), F32)
     ids = iota((BUCKETS, 1), 0)
     for b in range(BUCKETS):
         here = jnp.sum(jnp.where(ids == b, tiles, 0.0))
         before = before + jnp.where(ids > b, here, 0.0)
-    for b in range(BUCKETS):
-        start_ref[0, b] = jnp.sum(jnp.where(ids == b, before, 0.0)).astype(jnp.int32)
-    start_ref[0, BUCKETS] = jnp.sum(tiles).astype(jnp.int32)
+    tile_ids = iota((BUCKETS, CAP), 1).astype(F32)
+    of_tile = jnp.sum(jnp.where(tile_ids >= before + tiles, 1.0, 0.0), axis=0, keepdims=True)
+    used = jnp.sum(tiles)
+    of_tile = jnp.where(
+        iota((1, CAP), 1) == CAP - 1, used, jnp.minimum(of_tile, BUCKETS - 1.0)
+    )
+    bucket_ref[...] = of_tile.astype(jnp.int32)
+    used = used.astype(jnp.int32)
     offsets = before * float(SUB)
 
     acc_ref[...] = jnp.zeros_like(acc_ref)
@@ -321,113 +407,115 @@
         low = one_hot(iota((CAP, CHUNK), 0) == (pos & 127))
         inside = (cell & (ROWS * NY - 1)).astype(F32)
         pieces = []
-        for value in [inside] + [row_of(recv_ref, f, c) for f in range(1, 6)]:
+        for value in [inside] + [row_of(recv_ref, f, c) for f in range(1, 5)]:
             for part in parts_of(value, 2):
                 pieces.append(low * part)
         acc_ref[...] += nt(high, jnp.concatenate(pieces, axis=0))
         return carry
 
-    lax.fori_loop(0, chunks, sort_body, 0)
+    lax.fori_loop(0, chunks, sort_body, 0, unroll=2)
     for f in range(SORT_PARTS // 2):
         sorted_ref[f] = (
             acc_ref[:, 2 * f * CAP : (2 * f + 1) * CAP]
             + acc_ref[:, (2 * f + 1) * CAP : (2 * f + 2) * CAP]
         )
 
-    def bucket_body(b, carry):
-        def tile_body(t, total):
-            def row(f):
-                return jnp.concatenate(
-                    [sorted_ref[f, pl.ds(2 * t, 1), :], sorted_ref[f, pl.ds(2 * t + 1, 1), :]],
-                    axis=1,
-                )
-
-            cell = row(0).astype(jnp.int32)
-            hot = one_hot(iota((ROWS, SUB), 0) == (cell >> 8))
-            y = cell & (NY - 1)
+    bucket_rows = bucket_ref[...].astype(F32)
+    tile_lane = iota((1, CAP), 1)
+    forcing_ref[...] = jnp.zeros_like(forcing_ref)
+
+    def tile_body(i, carry):
+        for t in range(4):
+            t = 4 * i + t
+            cell, y, w, d = tile_rows(sorted_ref, t)
+            level_x = iota((ROWS, SUB), 0)
+            hot = short_hot(level_x, cell >> 8)
+            next_hot = short_hot(level_x, (cell >> 8) + 1)
             spots = iota((NY, SUB), 0)
-            here = one_hot(spots == lane_of(y))
-            above = one_hot(spots == lane_of(y + 1))
-            d = row(5)
-            w = [parts_of(row(1 + i) * d, 2) for i in range(4)]
-            stacked = jnp.concatenate(
-                [
-                    jnp.concatenate([here * w[0][p] + above * w[2][p] for p in range(2)], axis=1),
-                    jnp.concatenate([here * w[1][p] + above * w[3][p] for p in range(2)], axis=1),
-                ],
-                axis=0,
+            here = short_hot(spots, lane_of(y))
+            above = short_hot(spots, lane_of(y + 1))
+            w = [parts_of(x * d, 2) for x in w]
+            stacked = [here * w[0][p] + above * w[2][p] for p in range(2)]
+            stacked += [here * w[1][p] + above * w[3][p] for p in range(2)]
+            added = nt(
+                jnp.concatenate([hot, hot, next_hot, next_hot], axis=1),
+                jnp.concatenate(stacked, axis=1),
             )
-            return total + nt(jnp.concatenate([hot, hot], axis=1), stacked)
-
-        total = lax.fori_loop(
-            start_ref[0, b], start_ref[0, b + 1], tile_body, jnp.zeros((ROWS, 2 * NY), F32)
+            bucket = jnp.sum(jnp.where(tile_lane == t, bucket_rows, 0.0)).astype(jnp.int32)
+            forcing_ref[bucket] += added
+        return carry
+
+    lax.fori_loop(0, (used + 3) // 4, tile_body, 0)
+
+
+def tile_rows(sorted_ref, t):
+    def row(f):
+        return jnp.concatenate(
+            [sorted_ref[f, pl.ds(2 * t, 1), :], sorted_ref[f, pl.ds(2 * t + 1, 1), :]], axis=1
         )
-        forcing_ref[b] = total[:, :NY] + pltpu.roll(total[:, NY:], 1, 0)
-        return carry
-
-    lax.fori_loop(0, BUCKETS, bucket_body, 0)
+
+    cell = row(0).astype(jnp.int32)
+    w = [row(1), row(2), row(3)]
+    w.append(1.0 - w[0] - w[1] - w[2])
+    return cell, cell & (NY - 1), w, row(4)
 
 
 def gather_kernel(
-    start_ref, state_ref, sorted_ref, pos_ref, recv_ref, own_ref, out_ref, value_ref
+    bucket_ref, state_ref, sorted_ref, pos_ref, recv_ref, own_ref, out_ref, value_ref, table_ref
 ):
     devices = recv_ref.shape[0]
     chunks = devices * CAP // CHUNK
     value_ref[...] = jnp.zeros_like(value_ref)
 
-    def bucket_body(b, carry):
+    def table_body(b, carry):
         turned = state_ref[b].T
         shifted = pltpu.roll(turned, ROWS - 1, 1)
-        table = jnp.concatenate(
+        table_ref[b] = jnp.concatenate(
             [
                 jnp.concatenate(parts_of(turned, 2), axis=1),
                 jnp.concatenate(parts_of(shifted, 2), axis=1),
             ],
             axis=0,
         )
-
-        def tile_body(t, carry):
-            def row(f):
-                return jnp.concatenate(
-                    [sorted_ref[f, pl.ds(2 * t, 1), :], sorted_ref[f, pl.ds(2 * t + 1, 1), :]],
-                    axis=1,
-                )
-
-            cell = row(0).astype(jnp.int32)
+        return carry
+
+    lax.fori_loop(0, BUCKETS, table_body, 0)
+
+    def tile_body(i, carry):
+        for t in range(4):
+            t = 4 * i + t
+            cell, y, w, _ = tile_rows(sorted_ref, t)
             hot = one_hot(iota((ROWS, SUB), 0) == (cell >> 8))
-            y = cell & (NY - 1)
             spots = iota((NY, SUB), 0)
             here = spots == lane_of(y)
             above = spots == lane_of(y + 1)
-            got = nn(table, jnp.concatenate([hot, hot], axis=0))
-            first = jnp.where(here, row(1), jnp.where(above, row(3), 0.0))
-            second = jnp.where(here, row(2), jnp.where(above, row(4), 0.0))
-            value = jnp.sum(first * got[:NY] + second * got[NY:], axis=0, keepdims=True)
-            value_ref[pl.ds(2 * t, 1), :] = value[:, :CAP]
-            value_ref[pl.ds(2 * t + 1, 1), :] = value[:, CAP:]
-            return carry
-
-        return lax.fori_loop(start_ref[0, b], start_ref[0, b + 1], tile_body, carry)
-
-    lax.fori_loop(0, BUCKETS, bucket_body, 0)
+            got = nn(table_ref[bucket_ref[0, t]], jnp.concatenate([hot, hot], axis=0))
+            first = jnp.where(here, w[0], jnp.where(above, w[2], 0.0))
+            second = jnp.where(here, w[1], jnp.where(above, w[3], 0.0))
+            value_ref[pl.ds(t, 1), :] = jnp.sum(
+                first * got[:NY] + second * got[NY:], axis=0, keepdims=True
+            )
+        return carry
+
+    lax.fori_loop(0, (bucket_ref[0, CAP - 1] + 3) // 4, tile_body, 0)
     table = jnp.concatenate(parts_of(value_ref[...].T, 2), axis=1)
     depth = value_ref.shape[0]
 
     def unsort_body(c, carry):
         pos = pos_ref[pl.ds(c, 1), :]
-        high = one_hot(iota((depth, CHUNK), 0) == (pos >> 7))
+        high = one_hot(iota((depth, CHUNK), 0) == (pos >> 8))
         got = nn(table, jnp.concatenate([high, high], axis=0))
-        low = iota((CAP, CHUNK), 0) == (pos & 127)
+        low = iota((SUB, CHUNK), 0) == (pos & (SUB - 1))
         row = jnp.sum(jnp.where(low, got, 0.0), axis=0, keepdims=True)
         per = CHUNK // CAP
         block = jnp.concatenate([row[:, i * CAP : (i + 1) * CAP] for i in range(per)], axis=0)
         out_ref[pl.ds(pl.multiple_of(c * per, per), per), :CAP] = block
         return carry
 
-    lax.fori_loop(0, chunks, unsort_body, 0)
-    d = recv_ref[:, 5, :]
-    r = recv_ref[:, 6, :]
-    image = out_ref[:, :CAP] + recv_ref[:, 7, :] * d
+    lax.fori_loop(0, chunks, unsort_body, 0, unroll=2)
+    d = recv_ref[:, 4, :]
+    r = recv_ref[:, 5, :]
+    image = out_ref[:, :CAP] + recv_ref[:, 6, :] * d
     out_ref[:, :CAP] = image
     own = own_ref[...]
     lane = iota((1, CAP), 1)
@@ -448,16 +536,58 @@
     dual_out,
     res_out,
     dir_out,
+    halfway,
     landing,
     send_sem,
     recv_sem,
 ):
-    devices = out_ref.shape[0]
-    me = my_index()
-    greet_all(me)
-    await_all()
-    send_all(me, out_ref, landing, send_sem, recv_sem)
-    receive_all(landing, recv_sem)
+    g = lax.axis_index("tm")
+    t = lax.axis_index("space")
+    groups = lax.axis_size("tm")
+    strips = lax.axis_size("space")
+    devices = groups * strips
+
+    barrier = pltpu.get_barrier_semaphore()
+    for step in range(1, groups):
+        pl.semaphore_signal(
+            barrier, inc=1, device_id=(around(g, step, groups), t), device_id_type=MESH
+        )
+
+    def greet(i, carry):
+        other = (g, around(t, i, strips))
+        pl.semaphore_signal(barrier, inc=1, device_id=other, device_id_type=MESH)
+        return carry
+
+    lax.fori_loop(1, strips, greet, 0, unroll=True)
+    pl.semaphore_wait(barrier, groups + strips - 2)
+
+    def along_space(i, carry):
+        strip = around(t, i, strips)
+        pltpu.make_async_remote_copy(
+            src_ref=out_ref.at[:, strip],
+            dst_ref=halfway.at[:, strip_of(t)],
+            send_sem=send_sem.at[0],
+            recv_sem=recv_sem.at[0],
+            device_id=(g, strip),
+            device_id_type=MESH,
+        ).start()
+        return carry
+
+    lax.fori_loop(1, strips, along_space, 0, unroll=True)
+    pltpu.make_async_copy(out_ref.at[:, t], halfway.at[:, strip_of(t)], recv_sem.at[0]).start()
+    pltpu.make_async_copy(halfway, halfway, recv_sem.at[0]).wait()
+    for step in range(1, groups):
+        group = around(g, step, groups)
+        pltpu.make_async_remote_copy(
+            src_ref=halfway.at[group],
+            dst_ref=landing.at[g],
+            send_sem=send_sem.at[1],
+            recv_sem=recv_sem.at[1],
+            device_id=(group, t),
+            device_id_type=MESH,
+        ).start()
+    pltpu.make_async_copy(halfway.at[g], landing.at[g], recv_sem.at[1]).start()
+    pltpu.make_async_copy(landing, landing, recv_sem.at[1]).wait()
     returned = landing[...].reshape(devices, 2 * CAP)
     sums = jnp.sum(returned[:, CAP:], axis=0, keepdims=True)
     lane = iota((1, CAP), 1)
@@ -468,17 +598,21 @@
     norm_next = norm_now - 2.0 * step * cross + step * step * square
     ratio = norm_next / norm_now
     table = jnp.concatenate(parts_of(returned[:, :CAP].T, 2), axis=1)
-    for c in range(route_ref.shape[0]):
-        hot = one_hot(iota((devices, CHUNK), 0) == route_ref[c : c + 1, :])
+    for c in range(route_ref.shape[1] // CHUNK):
+        lanes = slice(c * CHUNK, (c + 1) * CHUNK)
+        hot = one_hot(iota((devices, CHUNK), 0) == route_ref[:, lanes])
         got = nn(table, jnp.concatenate([hot, hot], axis=0))
-        mask = iota((CAP, CHUNK), 0) == rank_ref[c : c + 1, :]
+        mask = iota((CAP, CHUNK), 0) == rank_ref[:, lanes]
         image = jnp.sum(jnp.where(mask, got, 0.0), axis=0, keepdims=True)
-        d = d_ref[c : c + 1, :]
-        res = r_ref[c : c + 1, :] - step * image
-        dual_out[c : c + 1, :] = dual_ref[c : c + 1, :] + step * d
-        res_out[c : c + 1, :] = res
-        dir_out[c : c + 1, :] = res + ratio * d
-    finish_sends(out_ref, send_sem)
+        d = d_ref[:, lanes]
+        res = r_ref[:, lanes] - step * image
+        dual_out[:, lanes] = dual_ref[:, lanes] + step * d
+        res_out[:, lanes] = res
+        dir_out[:, lanes] = res + ratio * d
+    rest = out_ref.at[:, pl.ds(0, strips - 1)]
+    pltpu.make_async_copy(rest, rest, send_sem.at[0]).wait()
+    rest = halfway.at[pl.ds(0, groups - 1)]
+    pltpu.make_async_copy(rest, rest, send_sem.at[1]).wait()
 
 
 def back(x):
@@ -492,9 +626,12 @@
 def sweep_kernel(
     forcing_ref,
     coef,
+    coupling_hbm,
+    scale_hbm,
+    state_ref,
     coupling_ref,
     scale_ref,
-    state_ref,
+    scalar_sem,
     hop_a,
     hop_x,
     fin_a,
@@ -527,13 +664,14 @@
     t = lax.axis_index("space")
     groups = lax.axis_size("tm")
     strips = lax.axis_size("space")
-    left = (g, lax.rem(t + strips - 1, strips))
-    right = (g, lax.rem(t + 1, strips))
+    strip = strip_of(t)
+    left = (g, strip_of(lax.rem(strip + strips - 1, strips)))
+    right = (g, strip_of(lax.rem(strip + 1, strips)))
     later = (lax.rem(g + 1, groups), t)
     earlier = (lax.rem(g + groups - 1, groups), t)
     sides = (left, right)
-    first_strip = t == 0
-    last_strip = t == strips - 1
+    first_strip = strip == 0
+    last_strip = strip == strips - 1
     last_group = g == groups - 1
     first_group = g == 0
 
@@ -541,6 +679,10 @@
     for other in (left, right, later, earlier):
         pl.semaphore_signal(barrier, inc=1, device_id=other, device_id_type=MESH)
 
+    coupling_fetch = pltpu.make_async_copy(coupling_hbm, coupling_ref, scalar_sem.at[0])
+    scale_fetch = pltpu.make_async_copy(scale_hbm, scale_ref, scalar_sem.at[1])
+    coupling_fetch.start()
+    scale_fetch.start()
     pl.semaphore_wait(barrier, 4)
 
     def to_side(src, dst, sems, side, *idx):
@@ -628,6 +770,8 @@
         lax.fori_loop(0, LEV, early, 0)
 
     inside = inside_grid(first_strip, last_strip)
+    coupling_fetch.wait()
+    scale_fetch.wait()
     mix = [[coupling_step * coupling_ref[v, w] for w in range(NV)] for v in range(NV)]
 
     def adjoint_level(u, l, rows):
@@ -727,7 +871,7 @@
         def _():
             await_sides(cov_in, cov_sem, l)
             for v, tile in enumerate(join(cov_in, l, 0)):
-                scale = scale_ref[v, l]
+                scale = scale_ref[0, v, l]
                 ext = jnp.concatenate([fin_a[l, v], tile], axis=0) * (keep * scale)
                 ext = 0.5 * ext + 0.25 * (pltpu.roll(ext, 1, 0) + pltpu.roll(ext, EXT - 1, 0))
                 ext = ext * keep
@@ -828,9 +972,14 @@
     return pl.pallas_call(
         sweep_kernel,
         out_shape=jax.ShapeDtypeStruct((STEPS, NV, LEV, CX, NY), F32),
-        in_specs=[VMEM, VMEM, SMEM, SMEM],
+        in_specs=[VMEM, VMEM, ANY, ANY],
         out_specs=VMEM,
-        scratch_shapes=[state] * 4
+        scratch_shapes=[
+            pltpu.SMEM((NV, NV), F32),
+            pltpu.SMEM((1, NV, LEV), F32),
+            pltpu.SemaphoreType.DMA((2,)),
+        ]
+        + [state] * 4
         + [edges] * 2
         + [wide_edges] * 2
         + [edges] * 4
@@ -856,21 +1005,11 @@
     coupling,
     cov_scale,
 ):
-    devices = lax.axis_size("tm") * lax.axis_size("space")
+    grid = (lax.axis_size("tm"), lax.axis_size("space"))
+    devices = grid[0] * grid[1]
     rows = direction.shape[0]
-    wide = (rows // CHUNK, CHUNK)
+    wide = (1, rows)
     route = obs_route.reshape(1, rows)
-    fields = jnp.concatenate(
-        [
-            (obs_cell + 1).astype(F32)[None],
-            obs_interp,
-            direction[None],
-            residual_dual[None],
-            obs_var[None],
-        ],
-        axis=0,
-    )
-    winds = jnp.concatenate([wind_x, wind_y], axis=0)
     tiles = pltpu.VMEM((devices, 8, CAP), F32)
     arrived, rank, coef = pl.pallas_call(
         route_kernel,
@@ -879,21 +1018,39 @@
             jax.ShapeDtypeStruct((1, rows), jnp.int32),
             jax.ShapeDtypeStruct((5, LEV, EXT, NY), F32),
         ),
-        in_specs=[VMEM, VMEM, VMEM],
+        in_specs=[ANY] * 8,
         out_specs=(VMEM, VMEM, VMEM),
         scratch_shapes=[
             tiles,
             tiles,
             pltpu.VMEM((devices, sum(PACK_PARTS) * CAP), F32),
             pltpu.VMEM((2, LEV, CX, NY), F32),
-            pltpu.VMEM((2, 2, LEV, CX, NY), F32),
+            pltpu.VMEM((3, 2, LEV, CX, NY), F32),
+            pltpu.VMEM((1, rows), jnp.int32),
+            pltpu.VMEM((1, rows), jnp.int32),
+            pltpu.VMEM((4, rows), F32),
+            pltpu.VMEM((1, rows), F32),
+            pltpu.VMEM((1, rows), F32),
+            pltpu.VMEM((1, rows), F32),
+            pltpu.VMEM((1, LEV, CX, NY), F32),
+            pltpu.VMEM((1, LEV, CX, NY), F32),
             pltpu.SemaphoreType.DMA,
             pltpu.SemaphoreType.DMA,
-            pltpu.SemaphoreType.DMA((2, 2)),
+            pltpu.SemaphoreType.DMA((2, 3)),
+            pltpu.SemaphoreType.DMA((8,)),
         ],
-        compiler_params=params(20, collective_id=2, has_side_effects=True),
+        compiler_params=params(58, collective_id=2, has_side_effects=True),
         name="route",
-    )(route, fields, winds)
+    )(
+        route,
+        obs_cell.reshape(1, rows),
+        obs_interp,
+        direction.reshape(1, rows),
+        residual_dual.reshape(1, rows),
+        obs_var.reshape(1, rows),
+        wind_x,
+        wind_y,
+    )
     slots = devices * CAP
     forcing, ordered, position, starts = pl.pallas_call(
         sort_scatter_kernel,
@@ -901,10 +1058,10 @@
             jax.ShapeDtypeStruct((BUCKETS, ROWS, NY), F32),
             jax.ShapeDtypeStruct((SORT_PARTS // 2, SORT_ROWS, CAP), F32),
             jax.ShapeDtypeStruct((slots // CHUNK, CHUNK), jnp.int32),
-            jax.ShapeDtypeStruct((1, BUCKETS + 1), jnp.int32),
+            jax.ShapeDtypeStruct((1, CAP), jnp.int32),
         ),
         in_specs=[VMEM],
-        out_specs=(VMEM, VMEM, VMEM, SMEM),
+        out_specs=(VMEM, VMEM, VMEM, VMEM),
         scratch_shapes=[
             pltpu.VMEM((slots // CHUNK, CHUNK), F32),
             pltpu.VMEM((SORT_ROWS, SORT_PARTS * CAP), F32),
@@ -912,13 +1069,16 @@
         compiler_params=params(20),
         name="sort_scatter",
     )(arrived)
-    states = sweeps(forcing.reshape(STEPS, NV, LEV, CX, NY), coef, coupling, cov_scale[0])
+    states = sweeps(forcing.reshape(STEPS, NV, LEV, CX, NY), coef, coupling, cov_scale)
     returning = pl.pallas_call(
         gather_kernel,
         out_shape=jax.ShapeDtypeStruct((devices, 2 * CAP), F32),
         in_specs=[SMEM, VMEM, VMEM, VMEM, VMEM, VMEM],
         out_specs=VMEM,
-        scratch_shapes=[pltpu.VMEM((256, CAP), F32)],
+        scratch_shapes=[
+            pltpu.VMEM((CAP, SUB), F32),
+            pltpu.VMEM((BUCKETS, 2 * NY, 2 * ROWS), BF16),
+        ],
         compiler_params=params(20),
         name="gather",
     )(
@@ -936,14 +1096,15 @@
         in_specs=[VMEM] * 6,
         out_specs=(VMEM, VMEM, VMEM),
         scratch_shapes=[
-            pltpu.VMEM((devices, 1, 2 * CAP), F32),
-            pltpu.SemaphoreType.DMA,
-            pltpu.SemaphoreType.DMA,
+            pltpu.VMEM(grid + (1, 2 * CAP), F32),
+            pltpu.VMEM(grid + (1, 2 * CAP), F32),
+            pltpu.SemaphoreType.DMA((2,)),
+            pltpu.SemaphoreType.DMA((2,)),
         ],
         compiler_params=params(12, collective_id=3, has_side_effects=True),
         name="final",
     )(
-        returning.reshape(devices, 1, 2 * CAP),
+        returning.reshape(grid + (1, 2 * CAP)),
         route.reshape(wide),
         rank.reshape(wide),
         dual_weights.reshape(wide),

time: 227 us -> 196 us (0.86)
  Pallas kernels: 219 us -> 189 us
  other arithmetic: 3.2 us -> 0 us
    pallas_call x1, Pallas kernels: 35 us -> 23.8 us  [per_device(): pl.pallas_call(sort_scatter_kernel, out_shape=(jax.ShapeDtypeStruct((BUCK...]
    pallas_call x1, Pallas kernels: 53.6 us -> 45.8 us  [per_device(): pl.pallas_call(final_kernel, out_shape=(out, out, out), in_specs=[VMEM] *...]
    pallas_call x1, Pallas kernels: 80.5 us -> 73 us  [sweeps(): pl.pallas_call(sweep_kernel, out_shape=jax.ShapeDtypeStruct((STEPS, NV, L...]
    unnamed x16 -> x23, local copies, waits for them, and re-layouts: 1.92 us -> 5.59 us
    pallas_call x1, Pallas kernels: 17.8 us -> 14.7 us  [per_device(): pl.pallas_call(gather_kernel, out_shape=jax.ShapeDtypeStruct((devices, 2...]
where the time goes in v3:
time: 196 us
  Pallas kernels  189 us (96%)
  local copies, waits for them, and re-layouts  5.72 us (3%)
    pallas_call x1, Pallas kernels, sweeps(): pl.pallas_call(sweep_kernel, out_shape=jax.ShapeDtypeStruct((STEPS, NV, L...  73 us
    pallas_call x1, Pallas kernels, per_device(): pl.pallas_call(final_kernel, out_shape=(out, out, out), in_specs=[VMEM] *...  45.8 us
    pallas_call x1, Pallas kernels, per_device(): pl.pallas_call(route_kernel, out_shape=(jax.ShapeDtypeStruct((devices, 8,...  31.9 us
    pallas_call x1, Pallas kernels, per_device(): pl.pallas_call(sort_scatter_kernel, out_shape=(jax.ShapeDtypeStruct((BUCK...  23.8 us
    pallas_call x1, Pallas kernels, per_device(): pl.pallas_call(gather_kernel, out_shape=jax.ShapeDtypeStruct((devices, 2...  14.7 us
    unnamed x23, local copies, waits for them, and re-layouts  5.59 us

profile of v3, /device:TPU:1, one launch (start us, length us, event | category | flops | bytes accessed | tf_op | source)
XLA Modules:
  0.0 195.6 jit_solution(4432890709559064579)
XLA Ops:
  0.6 31.9 %route.1 = (f32[128,8,128]{2,1,0:T(8,128)}, s32[1,8192]{1,0:T(1,128)}, f32[5,16,16,256]{3,2,1,0:T(8,128)}) custom-call(s32[1,8192]{1,0:T(1,128)} %bitcast.16, s32[1,8192]{1,0:T(1,128)} %bitcast.24, f32[4,8192]{1,0:T(4,128)} %interp_hbm.1, f32[1,8192]{1,0:T(1,128)} %bitcast.18, f32[1,8192]{1,0:T(1,128)} %bitcast.13, f32[1,8192]{1,0:T(1,128)} %bitcast.25, ...), custom_call_target="tpu_custom_call" | custom-call | tf_op jit(solution)/shard_map/route/pallas_call | solution.py:1014
  32.5 0.0 copy-start
  32.5 1.0 copy-done
  33.6 23.8 %sort_scatter.1 = (f32[16,128,256]{2,1,0:T(8,128)S(1)}, f32[5,160,128]{2,1,0:T(8,128)S(1)}, s32[16,1024]{1,0:T(8,128)S(1)}, s32[1,128]{1,0:T(1,128)S(1)}) custom-call(f32[128,8,128]{2,1,0:T(8,128)S(1)} %copy-done), custom_call_target="tpu_custom_call" | custom-call | tf_op jit(solution)/shard_map/sort_scatter/pallas_call | solution.py:1055
  57.3 0.0 copy-start.2
  57.4 1.3 copy-done.2
  58.7 0.7 copy-done.8
  59.3 0.7 copy-done.9
  60.0 73.0 %sweeps.1 = f32[4,4,16,8,256]{4,3,2,1,0:T(8,128)S(1)} custom-call(f32[4,4,16,8,256]{4,3,2,1,0:T(8,128)S(1)} %bitcast.12, f32[5,16,16,256]{3,2,1,0:T(8,128)S(1)} %copy-done.2, f32[4,4]{1,0:T(4,128)S(1)} %copy-done.8, f32[1,4,16]{2,1,0:T(4,128)S(1)} %copy-done.9), custom_call_target="tpu_custom_call" | custom-call | tf_op jit(solution)/shard_map/sweeps/pallas_call | solution.py:972
  133.1 0.0 copy-start.4
  133.1 0.0 copy-start.5
  133.1 0.0 copy-start.6
  133.1 0.0 copy-start.7
  133.1 0.0 copy-done.1
  133.1 0.0 copy-done.3
  133.2 14.7 %gather.1 = f32[128,256]{1,0:T(8,128)S(1)} custom-call(s32[1,128]{1,0:T(1,128)S(1)} %get-tuple-element.14.bucket_ref, f32[16,128,256]{2,1,0:T(8,128)S(1)} %bitcast.11, f32[5,160,128]{2,1,0:T(8,128)S(1)} %get-tuple-element.17.sorted_ref, s32[16,1024]{1,0:T(8,128)S(1)} %get-tuple-element.18.pos_ref, f32[128,8,128]{2,1,0:T(8,128)S(1)} %copy-done.1, ...), custom_call_target="tpu_custom_call" | custom-call | tf_op jit(solution)/shard_map/gather/pallas_call | solution.py:1073
  147.8 0.1 reshape.52.out_ref
  148.0 0.0 copy-done.4
  148.0 0.0 copy-done.5
  148.0 0.0 copy-done.6
  148.0 45.8 %final.1 = (f32[1,8192]{1,0:T(1,128)S(1)}, f32[1,8192]{1,0:T(1,128)S(1)}, f32[1,8192]{1,0:T(1,128)S(1)}) custom-call(f32[4,32,1,256]{3,2,1,0:T(1,128)S(1)} %reshape.52.out_ref, s32[1,8192]{1,0:T(1,128)S(1)} %bitcast.17, s32[1,8192]{1,0:T(1,128)S(1)} %copy-done.7, f32[1,8192]{1,0:T(1,128)S(1)} %bitcast.20, f32[1,8192]{1,0:T(1,128)S(1)} %bitcast.19, ...), custom_call_target="tpu_custom_call" | custom-call | tf_op jit(solution)/shard_map/final/pallas_call | solution.py:1093
  193.8 0.6 copy.17
  194.4 0.6 copy.18
  195.0 0.6 copy.19
  (5 shorter events, 0.0 us)
Async XLA Ops:
  32.5 1.0 copy-start
  57.3 1.3 copy-start.2
  58.7 0.7 copy-start.8
  59.3 0.7 copy-start.9
  60.0 73.1 %copy-start.1 = (f32[128,8,128]{2,1,0:T(8,128)S(1)}, f32[128,8,128]{2,1,0:T(8,128)}, u32[]{:S(2)}) copy-start(f32[128,8,128]{2,1,0:T(8,128)} %get-tuple-element.13.recv_ref) | copy-start | bytes 1572868
  60.0 73.1 %copy-start.3 = (f32[8192]{0:T(1024)S(1)}, f32[8192]{0:T(1024)}, u32[]{:S(2)}) copy-start(f32[8192]{0:T(1024)} %param.13) | copy-start | bytes 98308
  133.1 14.9 %copy-start.4 = (s32[8192,1]{0,1:T(1,128)S(1)}, s32[8192,1]{0,1:T(1,128)}, u32[]{:S(2)}) copy-start(s32[8192,1]{0,1:T(1,128)} %param.15) | copy-start | bytes 98308
  133.1 14.9 %copy-start.5 = (f32[8192]{0:T(1024)S(1)}, f32[8192]{0:T(1024)}, u32[]{:S(2)}) copy-start(f32[8192]{0:T(1024)} %param.12) | copy-start | bytes 98308
  133.1 14.9 %copy-start.6 = (f32[8192]{0:T(1024)S(1)}, f32[8192]{0:T(1024)}, u32[]{:S(2)}) copy-start(f32[8192]{0:T(1024)} %param.11) | copy-start | bytes 98308
  133.1 14.9 %copy-start.7 = (s32[1,8192]{1,0:T(1,128)S(1)}, s32[1,8192]{1,0:T(1,128)}, u32[]{:S(2)}) copy-start(s32[1,8192]{1,0:T(1,128)} %get-tuple-element.19.rank_ref) | copy-start | bytes 98308

commit v4 on v3

--- a/solution.py
+++ b/solution.py
@@ -187,6 +187,8 @@
     var_hbm,
     wind_x_hbm,
     wind_y_hbm,
+    coupling_hbm,
+    scale_hbm,
     arrived_ref,
     rank_ref,
     coef,
@@ -203,6 +205,8 @@
     var_ref,
     wind_x_ref,
     wind_y_ref,
+    coupling_ref,
+    scale_ref,
     send_sem,
     recv_sem,
     wind_sem,
@@ -220,6 +224,8 @@
                 (d_hbm, d_ref),
                 (r_hbm, r_ref),
                 (var_hbm, var_ref),
+                (coupling_hbm, coupling_ref),
+                (scale_hbm, scale_ref),
             )
         )
     ]
@@ -325,16 +331,19 @@
             )
             for i in range(2)
         ]
-        coef[0, l] = jnp.where(
+        coef[l] = jnp.where(
             inside, 1.0 - jnp.abs(wx) - jnp.abs(wy) - 4.0 * diffusion - 2.0 * vertical, 0.0
         )
-        coef[1, l] = jnp.where(west_ok, jnp.maximum(wx, 0.0) + diffusion, 0.0)
-        coef[2, l] = jnp.where(east_ok, jnp.maximum(-wx, 0.0) + diffusion, 0.0)
-        coef[3, l] = jnp.where(south_ok, jnp.maximum(wy, 0.0) + diffusion, 0.0)
-        coef[4, l] = jnp.where(north_ok, jnp.maximum(-wy, 0.0) + diffusion, 0.0)
+        coef[LEV + l] = jnp.where(west_ok, jnp.maximum(wx, 0.0) + diffusion, 0.0)
+        coef[2 * LEV + l] = jnp.where(east_ok, jnp.maximum(-wx, 0.0) + diffusion, 0.0)
+        coef[3 * LEV + l] = jnp.where(south_ok, jnp.maximum(wy, 0.0) + diffusion, 0.0)
+        coef[4 * LEV + l] = jnp.where(north_ok, jnp.maximum(-wy, 0.0) + diffusion, 0.0)
         return carry
 
     lax.fori_loop(0, LEV, coef_body, 0)
+    coef[5 * LEV] = jnp.zeros((EXT, NY), F32)
+    coef[5 * LEV, :NV, :NV] = coupling_ref[...]
+    coef[5 * LEV, CX : CX + NV, :LEV] = scale_ref[0]
     receive_all(landing, recv_sem)
     arrived_ref[...] = landing[...]
     to_strip(0).wait_send()
@@ -538,6 +547,7 @@
     dir_out,
     halfway,
     landing,
+    hot_ref,
     send_sem,
     recv_sem,
 ):
@@ -575,6 +585,10 @@
 
     lax.fori_loop(1, strips, along_space, 0, unroll=True)
     pltpu.make_async_copy(out_ref.at[:, t], halfway.at[:, strip_of(t)], recv_sem.at[0]).start()
+    chunks = route_ref.shape[1] // CHUNK
+    for c in range(chunks):
+        lanes = slice(c * CHUNK, (c + 1) * CHUNK)
+        hot_ref[c] = one_hot(iota((devices, CHUNK), 0) == route_ref[:, lanes])
     pltpu.make_async_copy(halfway, halfway, recv_sem.at[0]).wait()
     for step in range(1, groups):
         group = around(g, step, groups)
@@ -598,9 +612,9 @@
     norm_next = norm_now - 2.0 * step * cross + step * step * square
     ratio = norm_next / norm_now
     table = jnp.concatenate(parts_of(returned[:, :CAP].T, 2), axis=1)
-    for c in range(route_ref.shape[1] // CHUNK):
+    for c in range(chunks):
         lanes = slice(c * CHUNK, (c + 1) * CHUNK)
-        hot = one_hot(iota((devices, CHUNK), 0) == route_ref[:, lanes])
+        hot = hot_ref[c]
         got = nn(table, jnp.concatenate([hot, hot], axis=0))
         mask = iota((CAP, CHUNK), 0) == rank_ref[:, lanes]
         image = jnp.sum(jnp.where(mask, got, 0.0), axis=0, keepdims=True)
@@ -626,11 +640,8 @@
 def sweep_kernel(
     forcing_ref,
     coef,
-    coupling_hbm,
-    scale_hbm,
     state_ref,
-    coupling_ref,
-    scale_ref,
+    scalars,
     scalar_sem,
     hop_a,
     hop_x,
@@ -679,10 +690,8 @@
     for other in (left, right, later, earlier):
         pl.semaphore_signal(barrier, inc=1, device_id=other, device_id_type=MESH)
 
-    coupling_fetch = pltpu.make_async_copy(coupling_hbm, coupling_ref, scalar_sem.at[0])
-    scale_fetch = pltpu.make_async_copy(scale_hbm, scale_ref, scalar_sem.at[1])
-    coupling_fetch.start()
-    scale_fetch.start()
+    fetch = pltpu.make_async_copy(coef.at[5 * LEV, :, pl.ds(0, CAP)], scalars, scalar_sem)
+    fetch.start()
     pl.semaphore_wait(barrier, 4)
 
     def to_side(src, dst, sems, side, *idx):
@@ -770,12 +779,11 @@
         lax.fori_loop(0, LEV, early, 0)
 
     inside = inside_grid(first_strip, last_strip)
-    coupling_fetch.wait()
-    scale_fetch.wait()
-    mix = [[coupling_step * coupling_ref[v, w] for w in range(NV)] for v in range(NV)]
+    fetch.wait()
+    mix = [[coupling_step * scalars[v, w] for w in range(NV)] for v in range(NV)]
 
     def adjoint_level(u, l, rows):
-        c, w, e, s, n = [coef[i, l] for i in range(5)]
+        c, w, e, s, n = [coef[i * LEV + l] for i in range(5)]
         now = [u[l + 1, v] for v in range(NV)]
         out = []
         for v in range(NV):
@@ -790,7 +798,7 @@
         return out
 
     def forward_level(u, l, rows):
-        c, w, e, s, n = [coef[i, l][:rows] for i in range(5)]
+        c, w, e, s, n = [coef[i * LEV + l][:rows] for i in range(5)]
         now = [u[l + 1, v] for v in range(NV)]
         out = []
         for v in range(NV):
@@ -871,7 +879,7 @@
         def _():
             await_sides(cov_in, cov_sem, l)
             for v, tile in enumerate(join(cov_in, l, 0)):
-                scale = scale_ref[0, v, l]
+                scale = scalars[CX + v, l]
                 ext = jnp.concatenate([fin_a[l, v], tile], axis=0) * (keep * scale)
                 ext = 0.5 * ext + 0.25 * (pltpu.roll(ext, 1, 0) + pltpu.roll(ext, EXT - 1, 0))
                 ext = ext * keep
@@ -963,7 +971,7 @@
     lax.fori_loop(0, LEV, drain, 0)
 
 
-def sweeps(forcing, coef, coupling, scale):
+def sweeps(forcing, coef):
     state = pltpu.VMEM((LEV, NV, CX, NY), F32)
     padded = pltpu.VMEM((LEV + 2, NV, EXT, NY), F32)
     edges = pltpu.VMEM((2, LEV, 2, CX, NY), F32)
@@ -972,12 +980,11 @@
     return pl.pallas_call(
         sweep_kernel,
         out_shape=jax.ShapeDtypeStruct((STEPS, NV, LEV, CX, NY), F32),
-        in_specs=[VMEM, VMEM, ANY, ANY],
+        in_specs=[VMEM, VMEM],
         out_specs=VMEM,
         scratch_shapes=[
-            pltpu.SMEM((NV, NV), F32),
-            pltpu.SMEM((1, NV, LEV), F32),
-            pltpu.SemaphoreType.DMA((2,)),
+            pltpu.SMEM((EXT, CAP), F32),
+            pltpu.SemaphoreType.DMA,
         ]
         + [state] * 4
         + [edges] * 2
@@ -989,7 +996,7 @@
         + [levels] * 5,
         compiler_params=params(34, collective_id=1, has_side_effects=True),
         name="sweeps",
-    )(forcing, coef, coupling, scale)
+    )(forcing, coef)
 
 
 def per_device(
@@ -1016,9 +1023,9 @@
         out_shape=(
             jax.ShapeDtypeStruct((devices, 8, CAP), F32),
             jax.ShapeDtypeStruct((1, rows), jnp.int32),
-            jax.ShapeDtypeStruct((5, LEV, EXT, NY), F32),
+            jax.ShapeDtypeStruct((5 * LEV + 1, EXT, NY), F32),
         ),
-        in_specs=[ANY] * 8,
+        in_specs=[ANY] * 10,
         out_specs=(VMEM, VMEM, VMEM),
         scratch_shapes=[
             tiles,
@@ -1034,10 +1041,12 @@
             pltpu.VMEM((1, rows), F32),
             pltpu.VMEM((1, LEV, CX, NY), F32),
             pltpu.VMEM((1, LEV, CX, NY), F32),
+            pltpu.VMEM((NV, NV), F32),
+            pltpu.VMEM((1, NV, LEV), F32),
             pltpu.SemaphoreType.DMA,
             pltpu.SemaphoreType.DMA,
             pltpu.SemaphoreType.DMA((2, 3)),
-            pltpu.SemaphoreType.DMA((8,)),
+            pltpu.SemaphoreType.DMA((10,)),
         ],
         compiler_params=params(58, collective_id=2, has_side_effects=True),
         name="route",
@@ -1050,6 +1059,8 @@
         obs_var.reshape(1, rows),
         wind_x,
         wind_y,
+        coupling,
+        cov_scale,
     )
     slots = devices * CAP
     forcing, ordered, position, starts = pl.pallas_call(
@@ -1069,7 +1080,7 @@
         compiler_params=params(20),
         name="sort_scatter",
     )(arrived)
-    states = sweeps(forcing.reshape(STEPS, NV, LEV, CX, NY), coef, coupling, cov_scale)
+    states = sweeps(forcing.reshape(STEPS, NV, LEV, CX, NY), coef)
     returning = pl.pallas_call(
         gather_kernel,
         out_shape=jax.ShapeDtypeStruct((devices, 2 * CAP), F32),
@@ -1098,6 +1109,7 @@
         scratch_shapes=[
             pltpu.VMEM(grid + (1, 2 * CAP), F32),
             pltpu.VMEM(grid + (1, 2 * CAP), F32),
+            pltpu.VMEM((rows // CHUNK, devices, CHUNK), BF16),
             pltpu.SemaphoreType.DMA((2,)),
             pltpu.SemaphoreType.DMA((2,)),
         ],

time: 196 us -> 189 us (0.964)
  Pallas kernels: 189 us -> 183 us
    pallas_call x1, Pallas kernels: 73 us -> 66.6 us  [sweeps(): pl.pallas_call(sweep_kernel, out_shape=jax.ShapeDtypeStruct((STEPS, NV, L...]
    pallas_call x1, Pallas kernels: 45.8 us -> 39.9 us  [per_device(): pl.pallas_call(final_kernel, out_shape=(out, out, out), in_specs=[VMEM] *...]
    pallas_call x1, Pallas kernels: 23.8 us -> 27.2 us  [per_device(): pl.pallas_call(sort_scatter_kernel, out_shape=(jax.ShapeDtypeStruct((BUCK...]
    pallas_call x1, Pallas kernels: 14.7 us -> 17.7 us  [per_device(): pl.pallas_call(gather_kernel, out_shape=jax.ShapeDtypeStruct((devices, 2...]
    unnamed x23 -> x19, local copies, waits for them, and re-layouts: 5.59 us -> 4.23 us
where the time goes in v4:
time: 189 us
  Pallas kernels  183 us (97%)
  local copies, waits for them, and re-layouts  4.36 us (2%)
    pallas_call x1, Pallas kernels, sweeps(): pl.pallas_call(sweep_kernel, out_shape=jax.ShapeDtypeStruct((STEPS, NV, L...  66.6 us
    pallas_call x1, Pallas kernels, per_device(): pl.pallas_call(final_kernel, out_shape=(out, out, out), in_specs=[VMEM] *...  39.9 us
    pallas_call x1, Pallas kernels, per_device(): pl.pallas_call(route_kernel, out_shape=(jax.ShapeDtypeStruct((devices, 8,...  31.9 us
    pallas_call x1, Pallas kernels, per_device(): pl.pallas_call(sort_scatter_kernel, out_shape=(jax.ShapeDtypeStruct((BUCK...  27.2 us
    pallas_call x1, Pallas kernels, per_device(): pl.pallas_call(gather_kernel, out_shape=jax.ShapeDtypeStruct((devices, 2...  17.7 us
    unnamed x19, local copies, waits for them, and re-layouts  4.23 us

profile of v4, /device:TPU:1, one launch (start us, length us, event | category | flops | bytes accessed | tf_op | source)
XLA Modules:
  0.0 188.5 jit_solution(11668478793103376970)
XLA Ops:
  0.6 31.9 %route.1 = (f32[128,8,128]{2,1,0:T(8,128)}, s32[1,8192]{1,0:T(1,128)}, f32[81,16,256]{2,1,0:T(8,128)}) custom-call(s32[1,8192]{1,0:T(1,128)} %bitcast.16, s32[1,8192]{1,0:T(1,128)} %bitcast.24, f32[4,8192]{1,0:T(4,128)} %interp_hbm.1, f32[1,8192]{1,0:T(1,128)} %bitcast.18, f32[1,8192]{1,0:T(1,128)} %bitcast.13, f32[1,8192]{1,0:T(1,128)} %bitcast.25, ...), custom_call_target="tpu_custom_call" | custom-call | tf_op jit(solution)/shard_map/route/pallas_call | solution.py:1021
  32.6 0.0 copy-start
  32.6 1.0 copy-done
  33.6 27.2 %sort_scatter.1 = (f32[16,128,256]{2,1,0:T(8,128)S(1)}, f32[5,160,128]{2,1,0:T(8,128)S(1)}, s32[16,1024]{1,0:T(8,128)S(1)}, s32[1,128]{1,0:T(1,128)S(1)}) custom-call(f32[128,8,128]{2,1,0:T(8,128)S(1)} %copy-done), custom_call_target="tpu_custom_call" | custom-call | tf_op jit(solution)/shard_map/sort_scatter/pallas_call | solution.py:1066
  60.9 0.0 copy-start.2
  60.9 1.3 copy-done.2
  62.2 0.0 copy-start.1
  62.2 66.6 %sweeps.1 = f32[4,4,16,8,256]{4,3,2,1,0:T(8,128)S(1)} custom-call(f32[4,4,16,8,256]{4,3,2,1,0:T(8,128)S(1)} %bitcast.12, f32[81,16,256]{2,1,0:T(8,128)S(1)} %copy-done.2), custom_call_target="tpu_custom_call" | custom-call | tf_op jit(solution)/shard_map/sweeps/pallas_call | solution.py:980
  128.8 0.0 copy-start.4
  128.8 0.0 copy-start.5
  128.8 0.0 copy-start.6
  128.8 0.0 copy-start.7
  128.8 0.0 copy-done.1
  128.9 0.0 copy-done.3
  128.9 17.7 %gather.1 = f32[128,256]{1,0:T(8,128)S(1)} custom-call(s32[1,128]{1,0:T(1,128)S(1)} %get-tuple-element.14.bucket_ref, f32[16,128,256]{2,1,0:T(8,128)S(1)} %bitcast.11, f32[5,160,128]{2,1,0:T(8,128)S(1)} %get-tuple-element.17.sorted_ref, s32[16,1024]{1,0:T(8,128)S(1)} %get-tuple-element.18.pos_ref, f32[128,8,128]{2,1,0:T(8,128)S(1)} %copy-done.1, ...), custom_call_target="tpu_custom_call" | custom-call | tf_op jit(solution)/shard_map/gather/pallas_call | solution.py:1084
  146.6 0.1 reshape.52.out_ref
  146.7 0.0 copy-done.4
  146.7 0.0 copy-done.5
  146.8 0.0 copy-done.6
  146.8 0.0 copy-done.7
  146.8 39.9 %final.1 = (f32[1,8192]{1,0:T(1,128)S(1)}, f32[1,8192]{1,0:T(1,128)S(1)}, f32[1,8192]{1,0:T(1,128)S(1)}) custom-call(f32[4,32,1,256]{3,2,1,0:T(1,128)S(1)} %reshape.52.out_ref, s32[1,8192]{1,0:T(1,128)S(1)} %bitcast.17, s32[1,8192]{1,0:T(1,128)S(1)} %copy-done.7, f32[1,8192]{1,0:T(1,128)S(1)} %bitcast.20, f32[1,8192]{1,0:T(1,128)S(1)} %bitcast.19, ...), custom_call_target="tpu_custom_call" | custom-call | tf_op jit(solution)/shard_map/final/pallas_call | solution.py:1104
  186.7 0.6 copy.17
  187.3 0.6 copy.18
  187.9 0.6 copy.19
  (1 shorter events, 0.0 us)
Async XLA Ops:
  32.6 1.0 copy-start
  60.9 1.3 copy-start.2
  62.2 66.7 %copy-start.1 = (f32[128,8,128]{2,1,0:T(8,128)S(1)}, f32[128,8,128]{2,1,0:T(8,128)}, u32[]{:S(2)}) copy-start(f32[128,8,128]{2,1,0:T(8,128)} %get-tuple-element.13.recv_ref) | copy-start | bytes 1572868
  62.2 66.7 %copy-start.3 = (f32[8192]{0:T(1024)S(1)}, f32[8192]{0:T(1024)}, u32[]{:S(2)}) copy-start(f32[8192]{0:T(1024)} %param.13) | copy-start | bytes 98308
  128.8 17.9 %copy-start.4 = (s32[8192,1]{0,1:T(1,128)S(1)}, s32[8192,1]{0,1:T(1,128)}, u32[]{:S(2)}) copy-start(s32[8192,1]{0,1:T(1,128)} %param.15) | copy-start | bytes 98308
  128.8 17.9 %copy-start.5 = (f32[8192]{0:T(1024)S(1)}, f32[8192]{0:T(1024)}, u32[]{:S(2)}) copy-start(f32[8192]{0:T(1024)} %param.12) | copy-start | bytes 98308
  128.8 17.9 %copy-start.6 = (f32[8192]{0:T(1024)S(1)}, f32[8192]{0:T(1024)}, u32[]{:S(2)}) copy-start(f32[8192]{0:T(1024)} %param.11) | copy-start | bytes 98308
  128.8 17.9 %copy-start.7 = (s32[1,8192]{1,0:T(1,128)S(1)}, s32[1,8192]{1,0:T(1,128)}, u32[]{:S(2)}) copy-start(s32[1,8192]{1,0:T(1,128)} %get-tuple-element.19.rank_ref) | copy-start | bytes 98308

commit v5 on v4

--- a/solution.py
+++ b/solution.py
@@ -412,8 +412,8 @@
         pos = (offset + rank_ref[pl.ds(c, 1), :]).astype(jnp.int32)
         pos = jnp.where(cell < 0, -1, pos)
         pos_ref[pl.ds(c, 1), :] = pos
-        high = one_hot(iota((SORT_ROWS, CHUNK), 0) == (pos >> 7))
-        low = one_hot(iota((CAP, CHUNK), 0) == (pos & 127))
+        high = short_hot(iota((SORT_ROWS, CHUNK), 0), pos >> 7)
+        low = short_hot(iota((CAP, CHUNK), 0), pos & 127)
         inside = (cell & (ROWS * NY - 1)).astype(F32)
         pieces = []
         for value in [inside] + [row_of(recv_ref, f, c) for f in range(1, 5)]:
@@ -494,7 +494,7 @@
         for t in range(4):
             t = 4 * i + t
             cell, y, w, _ = tile_rows(sorted_ref, t)
-            hot = one_hot(iota((ROWS, SUB), 0) == (cell >> 8))
+            hot = short_hot(iota((ROWS, SUB), 0), cell >> 8)
             spots = iota((NY, SUB), 0)
             here = spots == lane_of(y)
             above = spots == lane_of(y + 1)
@@ -512,7 +512,7 @@
 
     def unsort_body(c, carry):
         pos = pos_ref[pl.ds(c, 1), :]
-        high = one_hot(iota((depth, CHUNK), 0) == (pos >> 8))
+        high = short_hot(iota((depth, CHUNK), 0), pos >> 8)
         got = nn(table, jnp.concatenate([high, high], axis=0))
         low = iota((SUB, CHUNK), 0) == (pos & (SUB - 1))
         row = jnp.sum(jnp.where(low, got, 0.0), axis=0, keepdims=True)

time: 189 us -> 191 us (1.011)
  Pallas kernels: 183 us -> 186 us
    pallas_call x1, Pallas kernels: 39.9 us -> 48.2 us  [per_device(): pl.pallas_call(final_kernel, out_shape=(out, out, out), in_specs=[VMEM] *...]
    pallas_call x1, Pallas kernels: 66.6 us -> 73.2 us  [sweeps(): pl.pallas_call(sweep_kernel, out_shape=jax.ShapeDtypeStruct((STEPS, NV, L...]
    pallas_call x1, Pallas kernels: 17.7 us -> 11.5 us  [per_device(): pl.pallas_call(gather_kernel, out_shape=jax.ShapeDtypeStruct((devices, 2...]
    pallas_call x1, Pallas kernels: 27.2 us -> 21 us  [per_device(): pl.pallas_call(sort_scatter_kernel, out_shape=(jax.ShapeDtypeStruct((BUCK...]
where the time goes in v5:
time: 191 us
  Pallas kernels  186 us (97%)
  local copies, waits for them, and re-layouts  4.36 us (2%)
    pallas_call x1, Pallas kernels, sweeps(): pl.pallas_call(sweep_kernel, out_shape=jax.ShapeDtypeStruct((STEPS, NV, L...  73.2 us
    pallas_call x1, Pallas kernels, per_device(): pl.pallas_call(final_kernel, out_shape=(out, out, out), in_specs=[VMEM] *...  48.2 us
    pallas_call x1, Pallas kernels, per_device(): pl.pallas_call(route_kernel, out_shape=(jax.ShapeDtypeStruct((devices, 8,...  31.9 us
    pallas_call x1, Pallas kernels, per_device(): pl.pallas_call(sort_scatter_kernel, out_shape=(jax.ShapeDtypeStruct((BUCK...  21 us
    pallas_call x1, Pallas kernels, per_device(): pl.pallas_call(gather_kernel, out_shape=jax.ShapeDtypeStruct((devices, 2...  11.5 us
    unnamed x19, local copies, waits for them, and re-layouts  4.23 us

profile of v5, /device:TPU:1, one launch (start us, length us, event | category | flops | bytes accessed | tf_op | source)
XLA Modules:
  0.0 191.0 jit_solution(14154266740660738480)
XLA Ops:
  0.6 31.9 %route.1 = (f32[128,8,128]{2,1,0:T(8,128)}, s32[1,8192]{1,0:T(1,128)}, f32[81,16,256]{2,1,0:T(8,128)}) custom-call(s32[1,8192]{1,0:T(1,128)} %bitcast.16, s32[1,8192]{1,0:T(1,128)} %bitcast.24, f32[4,8192]{1,0:T(4,128)} %interp_hbm.1, f32[1,8192]{1,0:T(1,128)} %bitcast.18, f32[1,8192]{1,0:T(1,128)} %bitcast.13, f32[1,8192]{1,0:T(1,128)} %bitcast.25, ...), custom_call_target="tpu_custom_call" | custom-call | tf_op jit(solution)/shard_map/route/pallas_call | solution.py:1021
  32.6 0.0 copy-start
  32.6 1.0 copy-done
  33.6 21.0 %sort_scatter.1 = (f32[16,128,256]{2,1,0:T(8,128)S(1)}, f32[5,160,128]{2,1,0:T(8,128)S(1)}, s32[16,1024]{1,0:T(8,128)S(1)}, s32[1,128]{1,0:T(1,128)S(1)}) custom-call(f32[128,8,128]{2,1,0:T(8,128)S(1)} %copy-done), custom_call_target="tpu_custom_call" | custom-call | tf_op jit(solution)/shard_map/sort_scatter/pallas_call | solution.py:1066
  54.6 0.0 copy-start.2
  54.6 1.3 copy-done.2
  56.0 0.0 copy-start.1
  56.0 73.2 %sweeps.1 = f32[4,4,16,8,256]{4,3,2,1,0:T(8,128)S(1)} custom-call(f32[4,4,16,8,256]{4,3,2,1,0:T(8,128)S(1)} %bitcast.12, f32[81,16,256]{2,1,0:T(8,128)S(1)} %copy-done.2), custom_call_target="tpu_custom_call" | custom-call | tf_op jit(solution)/shard_map/sweeps/pallas_call | solution.py:980
  129.2 0.0 copy-start.4
  129.2 0.0 copy-start.5
  129.2 0.0 copy-start.6
  129.2 0.0 copy-start.7
  129.2 0.0 copy-done.1
  129.2 0.0 copy-done.3
  129.3 11.5 %gather.1 = f32[128,256]{1,0:T(8,128)S(1)} custom-call(s32[1,128]{1,0:T(1,128)S(1)} %get-tuple-element.14.bucket_ref, f32[16,128,256]{2,1,0:T(8,128)S(1)} %bitcast.11, f32[5,160,128]{2,1,0:T(8,128)S(1)} %get-tuple-element.17.sorted_ref, s32[16,1024]{1,0:T(8,128)S(1)} %get-tuple-element.18.pos_ref, f32[128,8,128]{2,1,0:T(8,128)S(1)} %copy-done.1, ...), custom_call_target="tpu_custom_call" | custom-call | tf_op jit(solution)/shard_map/gather/pallas_call | solution.py:1084
  140.7 0.1 reshape.52.out_ref
  140.9 0.0 copy-done.4
  140.9 0.0 copy-done.5
  140.9 0.0 copy-done.6
  140.9 0.0 copy-done.7
  140.9 48.2 %final.1 = (f32[1,8192]{1,0:T(1,128)S(1)}, f32[1,8192]{1,0:T(1,128)S(1)}, f32[1,8192]{1,0:T(1,128)S(1)}) custom-call(f32[4,32,1,256]{3,2,1,0:T(1,128)S(1)} %reshape.52.out_ref, s32[1,8192]{1,0:T(1,128)S(1)} %bitcast.17, s32[1,8192]{1,0:T(1,128)S(1)} %copy-done.7, f32[1,8192]{1,0:T(1,128)S(1)} %bitcast.20, f32[1,8192]{1,0:T(1,128)S(1)} %bitcast.19, ...), custom_call_target="tpu_custom_call" | custom-call | tf_op jit(solution)/shard_map/final/pallas_call | solution.py:1104
  189.1 0.6 copy.17
  189.8 0.6 copy.18
  190.4 0.6 copy.19
  (1 shorter events, 0.0 us)
Async XLA Ops:
  32.6 1.0 copy-start
  54.6 1.3 copy-start.2
  56.0 73.3 %copy-start.1 = (f32[128,8,128]{2,1,0:T(8,128)S(1)}, f32[128,8,128]{2,1,0:T(8,128)}, u32[]{:S(2)}) copy-start(f32[128,8,128]{2,1,0:T(8,128)} %get-tuple-element.13.recv_ref) | copy-start | bytes 1572868
  56.0 73.3 %copy-start.3 = (f32[8192]{0:T(1024)S(1)}, f32[8192]{0:T(1024)}, u32[]{:S(2)}) copy-start(f32[8192]{0:T(1024)} %param.13) | copy-start | bytes 98308
  129.2 11.7 %copy-start.4 = (s32[8192,1]{0,1:T(1,128)S(1)}, s32[8192,1]{0,1:T(1,128)}, u32[]{:S(2)}) copy-start(s32[8192,1]{0,1:T(1,128)} %param.15) | copy-start | bytes 98308
  129.2 11.7 %copy-start.5 = (f32[8192]{0:T(1024)S(1)}, f32[8192]{0:T(1024)}, u32[]{:S(2)}) copy-start(f32[8192]{0:T(1024)} %param.12) | copy-start | bytes 98308
  129.2 11.7 %copy-start.6 = (f32[8192]{0:T(1024)S(1)}, f32[8192]{0:T(1024)}, u32[]{:S(2)}) copy-start(f32[8192]{0:T(1024)} %param.11) | copy-start | bytes 98308
  129.2 11.7 %copy-start.7 = (s32[1,8192]{1,0:T(1,128)S(1)}, s32[1,8192]{1,0:T(1,128)}, u32[]{:S(2)}) copy-start(s32[1,8192]{1,0:T(1,128)} %get-tuple-element.19.rank_ref) | copy-start | bytes 98308
